TPU v7x, 512 devices: a whole 4x8x8 slice. The times are simulated.
512 devices in a mesh: dom: 128 (over z, y, core), feat: 4 (over x).
Axes of the slice: x: 4, y: 8, z: 8, core: 2. Of those that a mesh axis runs over, the one named last changes fastest.
Arguments:
- features: bfloat16 [256, 262144], P('feat', 'dom'), may hold values from -6 to 6
- weight: bfloat16 [256, 256], P(None, 'feat'), may hold values from -0.375 to 0.375
- cotangent: bfloat16 [256, 262144], P('feat', 'dom'), may hold values from -6 to 6
- tile_values: bfloat16 [12288, 128, 128], P('dom'), may hold values from 0 to 0.07910156
- tile_rows: int32 [12288], P('dom'), may hold values from 0 to 15
- tile_cols: int32 [12288], P('dom'), may hold values from 0 to 71
- tile_count: int32 [128], P('dom'), may hold values from 32 to 96, as said below
- send_lists: int32 [128, 7, 8], P('dom'), may hold values from 0 to 15
- send_count: int32 [128, 7], P('dom'), may hold values from 1 to 8, as said below
Outputs:
- activated: bfloat16 [256, 262144], P('feat', 'dom')
- weight_grad: float32 [256, 256], P(None, 'feat')
- feature_grad: bfloat16 [256, 262144], P('feat', 'dom')
Inputs may be any that keep to these rules, and one draw needn't show every extreme that they name: `tile_count`: 96 in at least one partition. `send_count`: 8 in at least one partition in every round.
All inputs are finite; a program needn't handle non-finite values.
Results may differ from a plain program's by a relative error of at most 0.023.
Values may be sent and summed in bfloat16 or wider, within the bound.
A program may use at most 64 MiB of HBM per device.

v0:
```python
import jax
import jax.numpy as jnp
from jax import lax
from jax.sharding import PartitionSpec as P


def swapped(x, axis, distance):
    return lax.ppermute(x, axis, [(i, i ^ 1 << distance) for i in range(lax.axis_size(axis))])


def gelu_tanh(values):
    return jax.nn.gelu(values, approximate=True)


def slot_sum(form, contrib, onehot):
    high_part = contrib.astype(jnp.bfloat16)
    low_part = (contrib - high_part.astype(jnp.float32)).astype(jnp.bfloat16)
    first = jnp.einsum(form, high_part, onehot, preferred_element_type=jnp.float32)
    second = jnp.einsum(form, low_part, onehot, preferred_element_type=jnp.float32)
    return first + second


def local(
    features,
    weight,
    cotangent,
    tile_values,
    tile_rows,
    tile_cols,
    tile_count,
    send_lists,
    send_count,
):
    feat_rows, local_nodes = features.shape
    block_size = tile_values.shape[1]
    tile_slots = tile_values.shape[0]
    local_blocks = local_nodes // block_size
    rounds = send_lists.shape[1]
    per_round = send_lists.shape[2]
    highest = lax.Precision.HIGHEST
    blocks = features.reshape(feat_rows, local_blocks, block_size)
    lists = send_lists[0]
    keep_mask = (jnp.arange(per_round, dtype=jnp.int32)[None, :] < send_count[0][:, None]).astype(
        jnp.float32
    )
    received = []
    for level in range(rounds):
        outgoing = (
            jnp.take(blocks, lists[level], axis=1)
            * keep_mask[level].astype(jnp.bfloat16)[None, :, None]
        )
        received.append(swapped(outgoing, "dom", level))
    sources = jnp.concatenate([blocks] + received, axis=1)
    slot_total = sources.shape[1]
    live = (jnp.arange(tile_slots, dtype=jnp.int32) < tile_count[0]).astype(jnp.bfloat16)
    picked = jnp.take(sources, tile_cols, axis=1)
    contrib = jnp.einsum("ftc,trc->ftr", picked, tile_values, preferred_element_type=jnp.float32)
    row_onehot = (tile_rows[:, None] == jnp.arange(local_blocks, dtype=jnp.int32)[None, :]).astype(
        jnp.bfloat16
    ) * live[:, None]
    aggregated = slot_sum("ftr,tk->fkr", contrib, row_onehot)
    aggregated = aggregated.reshape(feat_rows, local_nodes).astype(jnp.bfloat16)
    full_agg = lax.all_gather(aggregated, "feat", axis=0, tiled=True)
    pre = lax.dot_general(
        weight, full_agg, (((0,), (0,)), ((), ())), preferred_element_type=jnp.float32
    )
    activated = gelu_tanh(pre).astype(jnp.bfloat16)
    pre_grad = jax.vjp(gelu_tanh, pre)[1](cotangent.astype(jnp.float32))[0].astype(jnp.bfloat16)
    weight_part = lax.dot_general(
        full_agg, pre_grad, (((1,), (1,)), ((), ())), preferred_element_type=jnp.float32
    )
    total_nodes = local_nodes * lax.axis_size("dom")
    weight_grad = lax.psum(weight_part, "dom") / jnp.sqrt(jnp.float32(total_nodes))
    agg_grad = lax.psum_scatter(
        jnp.dot(weight, pre_grad, preferred_element_type=jnp.float32).astype(jnp.bfloat16),
        "feat",
        scatter_dimension=0,
        tiled=True,
    ).astype(jnp.float32)
    agg_grad = agg_grad.astype(jnp.bfloat16).reshape(feat_rows, local_blocks, block_size)
    grad_picked = jnp.take(agg_grad, tile_rows, axis=1)
    grad_contrib = jnp.einsum(
        "ftr,trc->ftc", grad_picked, tile_values, preferred_element_type=jnp.float32
    )
    col_onehot = (tile_cols[:, None] == jnp.arange(slot_total, dtype=jnp.int32)[None, :]).astype(
        jnp.bfloat16
    ) * live[:, None]
    source_grad = slot_sum("ftc,ts->fsc", grad_contrib, col_onehot)
    local_grad = source_grad[:, :local_blocks]
    for level in range(rounds):
        start_slot = local_blocks + level * per_round
        outgoing_grad = source_grad[:, start_slot : start_slot + per_round]
        returned = swapped(outgoing_grad.astype(jnp.bfloat16), "dom", level).astype(
            outgoing_grad.dtype
        )
        place_onehot = (
            lists[level][:, None] == jnp.arange(local_blocks, dtype=jnp.int32)[None, :]
        ).astype(jnp.float32) * keep_mask[level][:, None]
        local_grad = local_grad + jnp.einsum(
            "fjc,jk->fkc", returned, place_onehot, precision=highest
        )
    feature_grad = local_grad.reshape(feat_rows, local_nodes).astype(jnp.bfloat16)
    return (activated, weight_grad, feature_grad)


def solution(mesh):
    return jax.shard_map(
        local,
        mesh=mesh,
        in_specs=(
            P("feat", "dom"),
            P(None, "feat"),
            P("feat", "dom"),
            P("dom", None, None),
            P("dom"),
            P("dom"),
            P("dom"),
            P("dom", None, None),
            P("dom", None),
        ),
        out_specs=(P("feat", "dom"), P(None, "feat"), P("feat", "dom")),
        check_vma=False,
    )
```

profile of v0, /device:TPU:1, one launch (start us, length us, event | category | flops | bytes accessed | tf_op | source)
XLA Modules:
  0.0 378.0 jit_solution(14081316857051577646)
XLA Ops:
  13.1 8.8 %collective-permute-start = (bf16[64,8,128]{2,0,1:T(8,128)(2,1)}, bf16[64,8,128]{2,0,1:T(8,128)(2,1)}, u32[]{:S(2)}, u32[]{:S(2)}) collective-permute-start(bf16[64,8,128]{2,0,1:T(8,128)(2,1)} %bitcast_multiply_fusion.6), channel_id=1, source_target_pairs={{0,4},{4,0},{8,12},{12,8},{16,20},{20,16},{24,28},{28,24},{32,36},... | collective-permute-start | bytes 393224 | tf_op jit(solution)/shard_map/ppermute | solution.py:8
  24.6 5.3 %collective-permute-start.6 = (bf16[64,8,128]{2,0,1:T(8,128)(2,1)}, bf16[64,8,128]{2,0,1:T(8,128)(2,1)}, u32[]{:S(2)}, u32[]{:S(2)}) collective-permute-start(bf16[64,8,128]{2,0,1:T(8,128)(2,1)} %bitcast_multiply_fusion), channel_id=1, source_target_pairs={{0,256},{4,260},{8,264},{12,268},{16,272},{20,276},{24,280},{28,28... | collective-permute-start | bytes 393224 | tf_op jit(solution)/shard_map/ppermute | solution.py:8
  32.4 3.2 collective-permute-start.1
  38.2 4.2 %collective-permute-start.2 = (bf16[64,8,128]{2,0,1:T(8,128)(2,1)}, bf16[64,8,128]{2,0,1:T(8,128)(2,1)}, u32[]{:S(2)}, u32[]{:S(2)}) collective-permute-start(bf16[64,8,128]{2,0,1:T(8,128)(2,1)} %bitcast_multiply_fusion.4), channel_id=1, source_target_pairs={{0,16},{4,20},{8,24},{12,28},{16,0},{20,4},{24,8},{28,12},{32,48},... | collective-permute-start | bytes 393224 | tf_op jit(solution)/shard_map/ppermute | solution.py:8
  45.0 4.7 %collective-permute-start.3 = (bf16[64,8,128]{2,0,1:T(8,128)(2,1)}, bf16[64,8,128]{2,0,1:T(8,128)(2,1)}, u32[]{:S(2)}, u32[]{:S(2)}) collective-permute-start(bf16[64,8,128]{2,0,1:T(8,128)(2,1)} %bitcast_multiply_fusion.3), channel_id=1, source_target_pairs={{0,32},{4,36},{8,40},{12,44},{16,48},{20,52},{24,56},{28,60},{32,0... | collective-permute-start | bytes 393224 | tf_op jit(solution)/shard_map/ppermute | solution.py:8
  50.8 1.7 constant_dynamic-update-slice_fusion.7
  58.6 3.1 collective-permute-start.4
  63.3 4.0 %collective-permute-start.5 = (bf16[64,8,128]{2,0,1:T(8,128)(2,1)S(1)}, bf16[64,8,128]{2,0,1:T(8,128)(2,1)S(1)}, u32[]{:S(2)}, u32[]{:S(2)}) collective-permute-start(bf16[64,8,128]{2,0,1:T(8,128)(2,1)S(1)} %bitcast_multiply_fusion.1), channel_id=1, source_target_pairs={{0,128},{4,132},{8,136},{12,140},{16,144},{20,148},{24,152},{28,15... | collective-permute-start | bytes 393224 | tf_op jit(solution)/shard_map/ppermute | solution.py:8
  68.9 1.6 constant_dynamic-update-slice_fusion.4
  74.5 1.6 constant_dynamic-update-slice_fusion
  76.1 3.3 gather_fusion
  79.4 3.7 fusion.1
  85.8 23.8 %all-gather.2.cloned.1.call-done = bf16[256,2048]{1,0:T(8,128)(2,1)} async-done(((bf16[64,2048]{1,0:T(8,128)(2,1)}), bf16[256,2048]{1,0:T(8,128)(2,1)}) %all-gather.2.cloned.1.call-update) | async-done | bytes 1048592 | tf_op jit(solution)/shard_map/all_gather | solution.py:63
  109.6 2.6 fusion.36
  113.7 2.3 copy.62
  117.3 2.3 fusion.122
  119.6 25.2 %reduce-scatter.4.cloned.1.call-done = bf16[64,2048]{1,0:T(8,128)(2,1)} async-done(((bf16[256,2048]{1,0:T(8,128)(2,1)}), bf16[64,2048]{1,0:T(8,128)(2,1)}) %reduce-scatter.4.cloned.1.call-update) | async-done | bytes 262160
  144.9 2.0 copy.63
  148.1 2.0 gather_fusion.1
  150.0 2.4 fusion
  153.7 2.7 fusion.121
  157.3 3.9 %collective-permute-start.7 = (bf16[64,8,128]{2,1,0:T(8,128)(2,1)}, bf16[64,8,128]{2,1,0:T(8,128)(2,1)}, u32[]{:S(2)}, u32[]{:S(2)}) collective-permute-start(bf16[64,8,128]{2,1,0:T(8,128)(2,1)} %get-tuple-element.28), channel_id=1, source_target_pairs={{0,4},{4,0},{8,12},{12,8},{16,20},{20,16},{24,28},{28,24},{32,36},... | collective-permute-start | bytes 393224 | tf_op jit(solution)/shard_map/ppermute | solution.py:8
  161.2 169.8 %all-reduce.2.cloned.1.call-done = f32[256,64]{0,1:T(8,128)} async-done(((f32[256,64]{0,1:T(8,128)}), f32[256,64]{0,1:T(8,128)}) %all-reduce.2.cloned.1.call-update) | async-done | bytes 65552 | tf_op jit(solution)/shard_map/psum | solution.py:73
  332.5 2.6 collective-permute-start.8
  335.1 2.2 collective-permute-start.13
  337.3 3.8 %collective-permute-start.12 = (bf16[64,8,128]{2,1,0:T(8,128)(2,1)S(1)}, bf16[64,8,128]{2,1,0:T(8,128)(2,1)S(1)}, u32[]{:S(2)}, u32[]{:S(2)}) collective-permute-start(bf16[64,8,128]{2,1,0:T(8,128)(2,1)S(1)} %get-tuple-element.24), channel_id=1, source_target_pairs={{0,128},{4,132},{8,136},{12,140},{16,144},{20,148},{24,152},{28,15... | collective-permute-start | bytes 393224 | tf_op jit(solution)/shard_map/ppermute | solution.py:8
  341.1 3.8 %collective-permute-start.11 = (bf16[64,8,128]{2,1,0:T(8,128)(2,1)}, bf16[64,8,128]{2,1,0:T(8,128)(2,1)S(1)}, u32[]{:S(2)}, u32[]{:S(2)}) collective-permute-start(bf16[64,8,128]{2,1,0:T(8,128)(2,1)} %get-tuple-element.25), channel_id=1, source_target_pairs={{0,64},{4,68},{8,72},{12,76},{16,80},{20,84},{24,88},{28,92},{32,9... | collective-permute-start | bytes 393224 | tf_op jit(solution)/shard_map/ppermute | solution.py:8
  344.9 2.2 collective-permute-start.9
  347.1 1.6 fusion.22
  348.8 7.3 %collective-permute-done.9 = bf16[64,8,128]{2,1,0:T(8,128)(2,1)S(1)} collective-permute-done((bf16[64,8,128]{2,1,0:T(8,128)(2,1)}, bf16[64,8,128]{2,1,0:T(8,128)(2,1)S(1)}, u32[]{:S(2)}, u32[]{:S(2)}) %collective-permute-start.9) | collective-permute-done | bytes 131104 | tf_op jit(solution)/shard_map/ppermute | solution.py:8
  356.1 1.9 collective-permute-start.10
  359.1 7.6 %collective-permute-done.10 = bf16[64,8,128]{2,1,0:T(8,128)(2,1)S(1)} collective-permute-done((bf16[64,8,128]{2,1,0:T(8,128)(2,1)}, bf16[64,8,128]{2,1,0:T(8,128)(2,1)S(1)}, u32[]{:S(2)}, u32[]{:S(2)}) %collective-permute-start.10) | collective-permute-done | bytes 131104 | tf_op jit(solution)/shard_map/ppermute | solution.py:8
  (94 shorter events, 46.2 us)
Async XLA Ops:
  7.2 72.2 %copy-start = (bf16[96,128,128]{2,1,0:T(8,128)(2,1)S(1)}, bf16[96,128,128]{2,1,0:T(8,128)(2,1)}, u32[]{:S(2)}) copy-start(bf16[96,128,128]{2,1,0:T(8,128)(2,1)} %param.14) | copy-start | bytes 9437188
  7.2 102.5 %all-gather.2.cloned.1.call-start = ((), (), s32[]{:S(2)}) async-start(), calls=%async_computation.1 | async-start | bytes 1310720 | tf_op jit(solution)/shard_map/all_gather | solution.py:63
  10.1 39.6 %copy-start.3 = (s32[96]{0:T(128)S(1)}, s32[96]{0:T(128)}, u32[]{:S(2)}) copy-start(s32[96]{0:T(128)} %param.16) | copy-start | bytes 1156
  13.1 45.5 %collective-permute-start = (bf16[64,8,128]{2,0,1:T(8,128)(2,1)}, bf16[64,8,128]{2,0,1:T(8,128)(2,1)}, u32[]{:S(2)}, u32[]{:S(2)}) collective-permute-start(bf16[64,8,128]{2,0,1:T(8,128)(2,1)} %bitcast_multiply_fusion.6), channel_id=1, source_target_pairs={{0,4},{4,0},{8,12},{12,8},{16,20},{20,16},{24,28},{28,24},{32,36},... | collective-permute-start | bytes 393224 | tf_op jit(solution)/shard_map/ppermute | solution.py:8
  24.6 50.0 %collective-permute-start.6 = (bf16[64,8,128]{2,0,1:T(8,128)(2,1)}, bf16[64,8,128]{2,0,1:T(8,128)(2,1)}, u32[]{:S(2)}, u32[]{:S(2)}) collective-permute-start(bf16[64,8,128]{2,0,1:T(8,128)(2,1)} %bitcast_multiply_fusion), channel_id=1, source_target_pairs={{0,256},{4,260},{8,264},{12,268},{16,272},{20,276},{24,280},{28,28... | collective-permute-start | bytes 393224 | tf_op jit(solution)/shard_map/ppermute | solution.py:8
  32.4 30.9 %collective-permute-start.1 = (bf16[64,8,128]{2,0,1:T(8,128)(2,1)}, bf16[64,8,128]{2,0,1:T(8,128)(2,1)}, u32[]{:S(2)}, u32[]{:S(2)}) collective-permute-start(bf16[64,8,128]{2,0,1:T(8,128)(2,1)} %bitcast_multiply_fusion.5), channel_id=1, source_target_pairs={{0,8},{4,12},{8,0},{12,4},{16,24},{20,28},{24,16},{28,20},{32,40},... | collective-permute-start | bytes 393224 | tf_op jit(solution)/shard_map/ppermute | solution.py:8
  38.2 30.7 %collective-permute-start.2 = (bf16[64,8,128]{2,0,1:T(8,128)(2,1)}, bf16[64,8,128]{2,0,1:T(8,128)(2,1)}, u32[]{:S(2)}, u32[]{:S(2)}) collective-permute-start(bf16[64,8,128]{2,0,1:T(8,128)(2,1)} %bitcast_multiply_fusion.4), channel_id=1, source_target_pairs={{0,16},{4,20},{8,24},{12,28},{16,0},{20,4},{24,8},{28,12},{32,48},... | collective-permute-start | bytes 393224 | tf_op jit(solution)/shard_map/ppermute | solution.py:8
  45.0 25.5 %collective-permute-start.3 = (bf16[64,8,128]{2,0,1:T(8,128)(2,1)}, bf16[64,8,128]{2,0,1:T(8,128)(2,1)}, u32[]{:S(2)}, u32[]{:S(2)}) collective-permute-start(bf16[64,8,128]{2,0,1:T(8,128)(2,1)} %bitcast_multiply_fusion.3), channel_id=1, source_target_pairs={{0,32},{4,36},{8,40},{12,44},{16,48},{20,52},{24,56},{28,60},{32,0... | collective-permute-start | bytes 393224 | tf_op jit(solution)/shard_map/ppermute | solution.py:8
  58.6 13.4 %collective-permute-start.4 = (bf16[64,8,128]{2,0,1:T(8,128)(2,1)S(1)}, bf16[64,8,128]{2,0,1:T(8,128)(2,1)S(1)}, u32[]{:S(2)}, u32[]{:S(2)}) collective-permute-start(bf16[64,8,128]{2,0,1:T(8,128)(2,1)S(1)} %bitcast_multiply_fusion.2), channel_id=1, source_target_pairs={{0,64},{4,68},{8,72},{12,76},{16,80},{20,84},{24,88},{28,92},{32,9... | collective-permute-start | bytes 393224 | tf_op jit(solution)/shard_map/ppermute | solution.py:8
  63.3 10.6 %collective-permute-start.5 = (bf16[64,8,128]{2,0,1:T(8,128)(2,1)S(1)}, bf16[64,8,128]{2,0,1:T(8,128)(2,1)S(1)}, u32[]{:S(2)}, u32[]{:S(2)}) collective-permute-start(bf16[64,8,128]{2,0,1:T(8,128)(2,1)S(1)} %bitcast_multiply_fusion.1), channel_id=1, source_target_pairs={{0,128},{4,132},{8,136},{12,140},{16,144},{20,148},{24,152},{28,15... | collective-permute-start | bytes 393224 | tf_op jit(solution)/shard_map/ppermute | solution.py:8
  76.1 3.3 copy-start.10
  79.4 3.7 copy-start.9
  84.0 25.7 %copy-start.1 = (bf16[256,64]{0,1:T(8,128)(2,1)S(1)}, bf16[256,64]{0,1:T(8,128)(2,1)}, u32[]{:S(2)}) copy-start(bf16[256,64]{0,1:T(8,128)(2,1)} %param.12) | copy-start | bytes 98308
  85.8 59.1 %reduce-scatter.4.cloned.1.call-start = ((), (), s32[]{:S(2)}) async-start(), calls=%async_computation.3 | async-start | bytes 1310720
  113.7 2.4 copy-start.2
  116.0 215.0 %all-reduce.2.cloned.1.call-start = ((), (), s32[]{:S(2)}) async-start(), calls=%async_computation.2 | async-start | bytes 131072 | tf_op jit(solution)/shard_map/psum | solution.py:73
  156.4 190.7 %copy-start.8 = (s32[8]{0:T(128)S(1)}, s32[8]{0:T(128)}, u32[]{:S(2)}) copy-start(s32[8]{0:T(128)} %get-tuple-element.49) | copy-start | bytes 100
  157.3 187.6 %collective-permute-start.7 = (bf16[64,8,128]{2,1,0:T(8,128)(2,1)}, bf16[64,8,128]{2,1,0:T(8,128)(2,1)}, u32[]{:S(2)}, u32[]{:S(2)}) collective-permute-start(bf16[64,8,128]{2,1,0:T(8,128)(2,1)} %get-tuple-element.28), channel_id=1, source_target_pairs={{0,4},{4,0},{8,12},{12,8},{16,20},{20,16},{24,28},{28,24},{32,36},... | collective-permute-start | bytes 393224 | tf_op jit(solution)/shard_map/ppermute | solution.py:8
  332.5 37.6 %collective-permute-start.8 = (bf16[64,8,128]{2,1,0:T(8,128)(2,1)S(1)}, bf16[64,8,128]{2,1,0:T(8,128)(2,1)S(1)}, u32[]{:S(2)}, u32[]{:S(2)}) collective-permute-start(bf16[64,8,128]{2,1,0:T(8,128)(2,1)S(1)} %get-tuple-element.22), channel_id=1, source_target_pairs={{0,8},{4,12},{8,0},{12,4},{16,24},{20,28},{24,16},{28,20},{32,40},... | collective-permute-start | bytes 393224 | tf_op jit(solution)/shard_map/ppermute | solution.py:8
  335.1 34.5 %collective-permute-start.13 = (bf16[64,8,128]{2,1,0:T(8,128)(2,1)S(1)}, bf16[64,8,128]{2,1,0:T(8,128)(2,1)S(1)}, u32[]{:S(2)}, u32[]{:S(2)}) collective-permute-start(bf16[64,8,128]{2,1,0:T(8,128)(2,1)S(1)} %get-tuple-element.23), channel_id=1, source_target_pairs={{0,256},{4,260},{8,264},{12,268},{16,272},{20,276},{24,280},{28,28... | collective-permute-start | bytes 393224 | tf_op jit(solution)/shard_map/ppermute | solution.py:8
  337.3 31.8 %collective-permute-start.12 = (bf16[64,8,128]{2,1,0:T(8,128)(2,1)S(1)}, bf16[64,8,128]{2,1,0:T(8,128)(2,1)S(1)}, u32[]{:S(2)}, u32[]{:S(2)}) collective-permute-start(bf16[64,8,128]{2,1,0:T(8,128)(2,1)S(1)} %get-tuple-element.24), channel_id=1, source_target_pairs={{0,128},{4,132},{8,136},{12,140},{16,144},{20,148},{24,152},{28,15... | collective-permute-start | bytes 393224 | tf_op jit(solution)/shard_map/ppermute | solution.py:8
  341.1 26.8 %collective-permute-start.11 = (bf16[64,8,128]{2,1,0:T(8,128)(2,1)}, bf16[64,8,128]{2,1,0:T(8,128)(2,1)S(1)}, u32[]{:S(2)}, u32[]{:S(2)}) collective-permute-start(bf16[64,8,128]{2,1,0:T(8,128)(2,1)} %get-tuple-element.25), channel_id=1, source_target_pairs={{0,64},{4,68},{8,72},{12,76},{16,80},{20,84},{24,88},{28,92},{32,9... | collective-permute-start | bytes 393224 | tf_op jit(solution)/shard_map/ppermute | solution.py:8
  344.9 11.1 %collective-permute-start.9 = (bf16[64,8,128]{2,1,0:T(8,128)(2,1)}, bf16[64,8,128]{2,1,0:T(8,128)(2,1)S(1)}, u32[]{:S(2)}, u32[]{:S(2)}) collective-permute-start(bf16[64,8,128]{2,1,0:T(8,128)(2,1)} %get-tuple-element.27), channel_id=1, source_target_pairs={{0,16},{4,20},{8,24},{12,28},{16,0},{20,4},{24,8},{28,12},{32,48},... | collective-permute-start | bytes 393224 | tf_op jit(solution)/shard_map/ppermute | solution.py:8
  347.1 21.9 %copy-start.5 = (s32[8]{0:T(128)S(1)}, s32[8]{0:T(128)}, u32[]{:S(2)}) copy-start(s32[8]{0:T(128)} %get-tuple-element.51) | copy-start | bytes 100
  347.1 21.9 %copy-start.7 = (f32[8]{0:T(128)S(1)}, f32[8]{0:T(128)}, u32[]{:S(2)}) copy-start(f32[8]{0:T(128)} %get-tuple-element.33) | copy-start | bytes 100
  348.8 20.8 %copy-start.4 = (s32[8]{0:T(128)S(1)}, s32[8]{0:T(128)}, u32[]{:S(2)}) copy-start(s32[8]{0:T(128)} %get-tuple-element.50) | copy-start | bytes 100
  348.8 20.8 %copy-start.6 = (f32[8]{0:T(128)S(1)}, f32[8]{0:T(128)}, u32[]{:S(2)}) copy-start(f32[8]{0:T(128)} %get-tuple-element.32) | copy-start | bytes 100
  356.1 10.6 %collective-permute-start.10 = (bf16[64,8,128]{2,1,0:T(8,128)(2,1)}, bf16[64,8,128]{2,1,0:T(8,128)(2,1)S(1)}, u32[]{:S(2)}, u32[]{:S(2)}) collective-permute-start(bf16[64,8,128]{2,1,0:T(8,128)(2,1)} %get-tuple-element.26), channel_id=1, source_target_pairs={{0,32},{4,36},{8,40},{12,44},{16,48},{20,52},{24,56},{28,60},{32,0... | collective-permute-start | bytes 393224 | tf_op jit(solution)/shard_map/ppermute | solution.py:8
Sparse Core Ops, SparseCore 0:
  85.9 23.7 all-gather.1
  116.1 28.6 reduce-scatter.3
  149.0 181.9 all-reduce.1
where the time goes:
time: 379 us; the launch traced here: 378 us
  waiting for transfers between devices  235 us (62%)
  starting transfers between devices  53.8 us (14%)
  local copies, waits for them, and re-layouts  31.5 us (8%)
  matrix products  24.9 us (7%)
  other arithmetic  17.9 us (5%)
  between operations  14.9 us (4%)
    psum x1, waiting for transfers between devices, local(): lax.psum(weight_part, 'dom') / jnp.sqrt(jnp.float32(total_nodes))  170 us
    ppermute x14, starting transfers between devices, swapped(): lax.ppermute(x, axis, [(i, i ^ 1 << distance) for i in range(lax.axis_siz...  53.7 us
    unnamed x4, waiting for transfers between devices  25.3 us
    all_gather x1, waiting for transfers between devices, local(): full_agg = lax.all_gather(aggregated, 'feat', axis=0, tiled=True)  23.8 us
    ppermute x14, waiting for transfers between devices, swapped(): lax.ppermute(x, axis, [(i, i ^ 1 << distance) for i in range(lax.axis_siz...  16.1 us
    unnamed x33, local copies, waits for them, and re-layouts  15.1 us
    mul x7, other arithmetic, local(): jnp.take(blocks, lists[level], axis=1)  8.71 us
  transfers between devices with their start and end apart: 17, of which 6 were waited for; matrix products, arithmetic and copies ran while one was open for 13% of the time, Pallas kernels for 0%

commit v1 on v0

v1 whole, which is shorter than its diff:
```python
import functools

import jax
import jax.numpy as jnp
from jax import lax
from jax.experimental import pallas as pl
from jax.experimental.pallas import tpu as pltpu
from jax.sharding import PartitionSpec as P

MESH = pl.DeviceIdType.MESH
CHUNKS = 2
UNROLL = 8
LANES = 128
GELU_C = 0.7978845608028654
GELU_A = 0.044715
F_PERM, F_SRC, F_KEEP, F_LAST, F_HAS = 0, 1, 2, 3, 4
B_PERM, B_SRC, B_KEEP, B_LAST, B_HAS = 5, 6, 7, 8, 9
E_PERM, E_KEEP, E_LAST, E_HAS = 10, 11, 12, 13


def sorted_order(key_row, other_row):
    shape = (LANES, LANES)
    ii = lax.broadcasted_iota(jnp.int32, shape, 0)
    jj = lax.broadcasted_iota(jnp.int32, shape, 1)
    key_l = jnp.broadcast_to(key_row, shape)
    other_l = jnp.broadcast_to(other_row, shape)
    key_s = jnp.sum(jnp.where(ii == jj, key_l, 0), axis=1, keepdims=True)
    other_s = jnp.sum(jnp.where(ii == jj, other_l, 0), axis=1, keepdims=True)
    same = jnp.where((key_l == key_s) & (jj < ii), 1, 0)
    dup_s = jnp.sum(same, axis=1, keepdims=True)
    rank_s = dup_s + jnp.sum(jnp.where(key_l < key_s, 1, 0), axis=1, keepdims=True)
    place = rank_s == jj
    perm = jnp.sum(jnp.where(place, ii, 0), axis=0, keepdims=True)
    other = jnp.sum(jnp.where(place, other_s, 0), axis=0, keepdims=True)
    keep = jnp.sum(jnp.where(place, jnp.minimum(dup_s, 1), 0), axis=0, keepdims=True)
    last = jnp.sum(jnp.where(key_s <= jj, 1, 0), axis=0, keepdims=True) - 1
    has = jnp.sum(jnp.where(key_s == jj, 1, 0), axis=0, keepdims=True)
    return perm, other, keep, jnp.maximum(last, 0), jnp.minimum(has, 1)


def kernel(
    cfg,
    x_hbm, w_hbm, cot_hbm, tiles_hbm, rows_s, cols_s, count_s, lists_s, sc_s,
    act_hbm, wgrad_ref, fg_hbm,
    *scratch,
):
    (H, FR, NODES, NB, T, R, SB, D, F, PLANE, Z) = cfg
    C = CHUNKS
    ROWS = FR // C
    HALO = R * SB
    NBQ = NB // F
    NQ = NODES // F
    refs = list(scratch)

    def take(n):
        out = refs[:n]
        del refs[:n]
        return out

    (xv, xb, tv, snd, aggS, aggG, cotG, wg, wfull, wt, pg, actS, agS) = take(13)
    src = take(C)
    gb = take(C)
    (buf, ret_s) = take(2)
    ret_r = take(C)
    (ebuf, fgv, wpS, wxR, wR, rsR, zR, finR, tab_v, tab_s) = take(10)
    (loc_sem, halo_sem, a2a_sem, w_sem, cot_sem, act_sem, ag_sem, ret_sem, wx_sem, rs_sem, z_sem, fin_sem) = take(12)

    dom = lax.axis_index("dom")
    me = lax.axis_index("feat")
    m = lax.rem(dom, PLANE)
    zi = dom // PLANE

    def dom_at(mm, zz):
        return zz * PLANE + mm

    barrier = pltpu.get_barrier_semaphore()
    for d in range(1, F):
        pl.semaphore_signal(barrier, inc=1, device_id=(dom, lax.rem(me + d, F)), device_id_type=MESH)

    def hello_plane(d, c):
        pl.semaphore_signal(
            barrier, inc=1, device_id=(dom_at(lax.rem(m + d, PLANE), zi), me), device_id_type=MESH
        )
        return c

    lax.fori_loop(1, PLANE, hello_plane, 0)

    def hello_z(d, c):
        pl.semaphore_signal(
            barrier, inc=1, device_id=(dom_at(m, lax.rem(zi + d, Z)), me), device_id_type=MESH
        )
        return c

    lax.fori_loop(1, Z, hello_z, 0)

    load_x = pltpu.make_async_copy(x_hbm, xv, loc_sem.at[0])
    load_x.start()
    load_t = pltpu.make_async_copy(tiles_hbm, tv, loc_sem.at[1])
    load_t.start()
    own_cot = pltpu.make_async_copy(
        cot_hbm.at[:, pl.ds(pl.multiple_of(me * NQ, LANES), NQ)],
        cotG.at[pl.ds(pl.multiple_of(me * FR, 16), FR), :],
        loc_sem.at[2],
    )
    own_cot.start()
    own_w = pltpu.make_async_copy(w_hbm, wg.at[me], loc_sem.at[3])
    own_w.start()
    load_x.wait()

    for k in range(NB):
        xb[k] = xv[:, k * LANES : (k + 1) * LANES]
    zero_block = jnp.zeros((FR, LANES), jnp.int32)
    for b in range(R):

        def fill(j, c, b=b):
            live = (zero_block + j < sc_s[0, b]).astype(jnp.float32)
            block = (xb[lists_s[0, b, j]].astype(jnp.float32) * live).astype(jnp.bfloat16)
            for h in range(C):
                snd[h, b * SB + j] = block[h * ROWS : (h + 1) * ROWS]
            return c

        lax.fori_loop(0, SB, fill, 0)

    pl.semaphore_wait(barrier, (F - 1) + (PLANE - 1) + (Z - 1))

    def halo_copy(h, b):
        return pltpu.make_async_remote_copy(
            src_ref=snd.at[h, pl.ds(b * SB, SB)],
            dst_ref=src[h].at[pl.ds(NB + b * SB, SB)],
            send_sem=halo_sem.at[0, h * R + b],
            recv_sem=halo_sem.at[1, h * R + b],
            device_id=(partner(b), me),
            device_id_type=MESH,
        )

    def partner(b):
        step = 1 << b
        bit = lax.rem(dom // step, 2)
        return dom + step - 2 * step * bit

    def feat_peer(d):
        return lax.rem(me + d, F)

    order = list(range(R))[::-1]
    sends = []
    halo = {}
    for b in order:
        halo[0, b] = halo_copy(0, b)
        halo[0, b].start()
    w_copies, cot_copies = [], []
    for d in range(1, F):
        q = feat_peer(d)
        cp = pltpu.make_async_remote_copy(
            src_ref=w_hbm,
            dst_ref=wg.at[me],
            send_sem=w_sem.at[0, d],
            recv_sem=w_sem.at[1, d],
            device_id=(dom, q),
            device_id_type=MESH,
        )
        cp.start()
        w_copies.append(cp)
        cp = pltpu.make_async_remote_copy(
            src_ref=cot_hbm.at[:, pl.ds(pl.multiple_of(q * NQ, LANES), NQ)],
            dst_ref=cotG.at[pl.ds(pl.multiple_of(me * FR, 16), FR), :],
            send_sem=cot_sem.at[0, d],
            recv_sem=cot_sem.at[1, d],
            device_id=(dom, q),
            device_id_type=MESH,
        )
        cp.start()
        cot_copies.append(cp)
    for h in range(1, C):
        for b in order:
            halo[h, b] = halo_copy(h, b)
            halo[h, b].start()

    lane = lax.broadcasted_iota(jnp.int32, (1, LANES), 1)

    def read_tile(t, c):
        r, k = c
        return jnp.where(lane == t, rows_s[t], r), jnp.where(lane == t, cols_s[t], k)

    zero_row = jnp.zeros((1, LANES), jnp.int32)
    rows_v, cols_v = lax.fori_loop(0, T, read_tile, (zero_row, zero_row))

    list_v = zero_row + (LANES - 1)
    for b in range(R):

        def read_entry(j, c, b=b):
            return jnp.where((lane == b * SB + j) & (zero_row + j < sc_s[0, b]), lists_s[0, b, j], c)

        list_v = lax.fori_loop(0, SB, read_entry, list_v)
    dead = lane >= count_s[0]
    fwd = sorted_order(jnp.where(dead, LANES - 1, rows_v), cols_v)
    bwd = sorted_order(jnp.where(dead, LANES - 1, cols_v), rows_v)
    ent = sorted_order(list_v, list_v)
    for place, row in zip(
        (F_PERM, F_SRC, F_KEEP, F_LAST, F_HAS, B_PERM, B_SRC, B_KEEP, B_LAST, B_HAS, E_PERM, E_KEEP, E_LAST, E_HAS),
        fwd + bwd + (ent[0],) + ent[2:],
    ):
        tab_v[pl.ds(place, 1), :] = row
    tab_v[pl.ds(14, 2), :] = jnp.zeros((2, LANES), jnp.int32)
    table = pltpu.make_async_copy(tab_v, tab_s, loc_sem.at[4])
    table.start()

    for k in range(NB):
        for h in range(C):
            src[h][k] = xb[k, h * ROWS : (h + 1) * ROWS]

    own_w.wait()
    for cp in w_copies:
        cp.wait_recv()
    wall = jnp.concatenate([wg[q].astype(jnp.float32) for q in range(F)], axis=1)
    wfull[...] = wall.astype(jnp.bfloat16)
    wt[...] = jnp.transpose(wall).astype(jnp.bfloat16)

    table.wait()
    load_t.wait()

    def tile_pass(source, perm, other, keep, contract):
        def body(i, run):
            for u in range(UNROLL):
                t = i * UNROLL + u
                part = lax.dot_general(
                    source[tab_s[other, t]],
                    tv[tab_s[perm, t]],
                    (((1,), (contract,)), ((), ())),
                    preferred_element_type=jnp.float32,
                )
                run = run * tab_s[keep, t].astype(jnp.float32) + part
                buf[t] = run
            return run

        lax.fori_loop(0, T // UNROLL, body, jnp.zeros((ROWS, LANES), jnp.float32))

    def segment(values, last, has, k):
        return values[tab_s[last, k]] * tab_s[has, k].astype(jnp.float32)

    a2a, a2a_own = [], []
    for h in range(C):
        for b in order:
            halo[h, b].wait_recv()
        tile_pass(src[h], F_PERM, F_SRC, F_KEEP, 1)
        for k in range(NB):
            aggS[h, k // NBQ, :, (k % NBQ) * LANES : (k % NBQ + 1) * LANES] = segment(
                buf, F_LAST, F_HAS, k
            ).astype(jnp.bfloat16)
        place = pl.ds(pl.multiple_of(me * FR + h * ROWS, 16), ROWS)
        for d in range(1, F):
            q = feat_peer(d)
            cp = pltpu.make_async_remote_copy(
                src_ref=aggS.at[h, q],
                dst_ref=aggG.at[place, :],
                send_sem=a2a_sem.at[0, h * F + d],
                recv_sem=a2a_sem.at[1, h * F + d],
                device_id=(dom, q),
                device_id_type=MESH,
            )
            cp.start()
            a2a.append(cp)
        cp = pltpu.make_async_copy(aggS.at[h, me], aggG.at[place, :], loc_sem.at[5 + h])
        cp.start()
        a2a_own.append(cp)

    own_cot.wait()
    for cp in cot_copies:
        cp.wait_recv()
    for cp in a2a_own:
        cp.wait()
    for cp in a2a:
        cp.wait_recv()

    def dense(q, c):
        here = pl.ds(pl.multiple_of(q * FR, 16), FR)
        pre = jnp.dot(wt[here, :], aggG[...], preferred_element_type=jnp.float32)
        square = pre * pre
        t = jnp.tanh(GELU_C * pre * (1.0 + GELU_A * square))
        half = 0.5 * (1.0 + t)
        actS[q] = (pre * half).astype(jnp.bfloat16)
        slope = half + (0.5 * GELU_C) * pre * (1.0 - t * t) * (1.0 + (3.0 * GELU_A) * square)
        pg[here, :] = (cotG[here, :].astype(jnp.float32) * slope).astype(jnp.bfloat16)
        return c

    lax.fori_loop(0, F, dense, 0)

    ag, ag_own = [], []
    for h in range(C):

        def agg_grad(q, c, h=h):
            here = pl.ds(pl.multiple_of(q * FR + h * ROWS, 16), ROWS)
            g = jnp.dot(wfull[here, :], pg[...], preferred_element_type=jnp.float32).astype(jnp.bfloat16)
            for k in range(NBQ):
                agS[h, q, k] = g[:, k * LANES : (k + 1) * LANES]
            return c

        lax.fori_loop(0, F, agg_grad, 0)
        place = pl.ds(me * NBQ, NBQ)
        for d in range(1, F):
            q = feat_peer(d)
            cp = pltpu.make_async_remote_copy(
                src_ref=agS.at[h, q],
                dst_ref=gb[h].at[place],
                send_sem=ag_sem.at[0, h * F + d],
                recv_sem=ag_sem.at[1, h * F + d],
                device_id=(dom, q),
                device_id_type=MESH,
            )
            cp.start()
            ag.append(cp)
        cp = pltpu.make_async_copy(agS.at[h, me], gb[h].at[place], loc_sem.at[5 + C + h])
        cp.start()
        ag_own.append(cp)

    place = pl.ds(pl.multiple_of(me * NQ, LANES), NQ)
    act = []
    for d in range(1, F):
        q = feat_peer(d)
        cp = pltpu.make_async_remote_copy(
            src_ref=actS.at[q],
            dst_ref=act_hbm.at[:, place],
            send_sem=act_sem.at[0, d],
            recv_sem=act_sem.at[1, d],
            device_id=(dom, q),
            device_id_type=MESH,
        )
        cp.start()
        act.append(cp)
    act_own = pltpu.make_async_copy(actS.at[me], act_hbm.at[:, place], loc_sem.at[5 + 2 * C])
    act_own.start()

    def weight_term(q, c):
        here = pl.ds(pl.multiple_of(q * FR, 16), FR)
        wpS[q] = lax.dot_general(
            pg[here, :], aggG[...], (((1,), (1,)), ((), ())), preferred_element_type=jnp.float32
        )
        return c

    lax.fori_loop(0, F, weight_term, 0)
    wx = []
    for d in range(1, F):
        cp = pltpu.make_async_remote_copy(
            src_ref=wpS.at[feat_peer(d)],
            dst_ref=wxR.at[d],
            send_sem=wx_sem.at[0, d],
            recv_sem=wx_sem.at[1, d],
            device_id=(dom, feat_peer(d)),
            device_id_type=MESH,
        )
        cp.start()
        wx.append(cp)

    def plane_copy(d, from_ref, to_ref, sem):
        mm = lax.rem(m + d, PLANE)
        return pltpu.make_async_remote_copy(
            src_ref=from_ref(mm),
            dst_ref=to_ref.at[m],
            send_sem=sem.at[0, d],
            recv_sem=sem.at[1, d],
            device_id=(dom_at(mm, zi), me),
            device_id_type=MESH,
        )

    def rs_copy(d):
        return plane_copy(d, lambda mm: wR.at[mm], rsR, rs_sem)

    def fin_copy(d):
        return plane_copy(d, lambda mm: finR.at[m], finR, fin_sem)

    def z_copy(d):
        return pltpu.make_async_remote_copy(
            src_ref=zR.at[zi],
            dst_ref=zR.at[zi],
            send_sem=z_sem.at[0, d],
            recv_sem=z_sem.at[1, d],
            device_id=(dom_at(m, lax.rem(zi + d, Z)), me),
            device_id_type=MESH,
        )

    def each(low, high, act_on):
        def body(d, c):
            act_on(d)
            return c

        lax.fori_loop(low, high, body, 0)

    across = H // LANES

    def reduce_feat():
        for cp in wx:
            cp.wait_recv()
        total = wpS[me]
        for d in range(1, F):
            total = total + wxR[d]
        for p in range(PLANE):
            wR[p] = total[8 * (p // across) : 8 * (p // across) + 8, LANES * (p % across) : LANES * (p % across + 1)]
        each(1, PLANE, lambda d: rs_copy(d).start())

    def reduce_plane():
        rsR[m] = wR[m]
        each(1, PLANE, lambda d: rs_copy(d).wait_recv())
        total = rsR[0]
        for p in range(1, PLANE):
            total = total + rsR[p]
        zR[zi] = total
        each(1, Z, lambda d: z_copy(d).start())

    def reduce_z():
        each(1, Z, lambda d: z_copy(d).wait_recv())
        total = zR[0]
        for p in range(1, Z):
            total = total + zR[p]
        finR[m] = total * (float(NODES * D) ** -0.5)
        each(1, PLANE, lambda d: fin_copy(d).start())

    def finish_weight():
        each(1, PLANE, lambda d: fin_copy(d).wait_recv())
        whole = jnp.concatenate(
            [
                jnp.concatenate([finR[r * across + a] for a in range(across)], axis=1)
                for r in range(FR // 8)
            ],
            axis=0,
        )
        wgrad_ref[...] = jnp.transpose(whole)

    def ret_copy(h, b):
        return pltpu.make_async_remote_copy(
            src_ref=ret_s.at[h, pl.ds(b * SB, SB)],
            dst_ref=ret_r[h].at[pl.ds(b * SB, SB)],
            send_sem=ret_sem.at[0, h * R + b],
            recv_sem=ret_sem.at[1, h * R + b],
            device_id=(partner(b), me),
            device_id_type=MESH,
        )

    ret = {}
    for h in range(C):
        ag_own[h].wait()
        for cp in ag[h * (F - 1) : (h + 1) * (F - 1)]:
            cp.wait_recv()
        tile_pass(gb[h], B_PERM, B_SRC, B_KEEP, 0)
        for b in order:
            for j in range(SB):
                s = b * SB + j
                ret_s[h, s] = segment(buf, B_LAST, B_HAS, NB + s).astype(jnp.bfloat16)
            ret[h, b] = ret_copy(h, b)
            ret[h, b].start()
        for k in range(NB):
            fgv[h, k] = segment(buf, B_LAST, B_HAS, k)
        if h == 0:
            reduce_feat()
    reduce_plane()

    outs = []
    for h in range(C):
        for b in order:
            ret[h, b].wait_recv()

        def gather_entry(e, run, h=h):
            run = run * tab_s[E_KEEP, e].astype(jnp.float32) + ret_r[h][tab_s[E_PERM, e]].astype(jnp.float32)
            ebuf[e] = run
            return run

        lax.fori_loop(0, HALO, gather_entry, jnp.zeros((ROWS, LANES), jnp.float32))
        for k in range(NB):
            xv[h * ROWS : (h + 1) * ROWS, k * LANES : (k + 1) * LANES] = (
                fgv[h, k] + segment(ebuf, E_LAST, E_HAS, k)
            ).astype(jnp.bfloat16)
        here = pl.ds(h * ROWS, ROWS)
        cp = pltpu.make_async_copy(xv.at[here, :], fg_hbm.at[here, :], loc_sem.at[6 + 2 * C + h])
        cp.start()
        outs.append(cp)
        if h == 0:
            reduce_z()
    finish_weight()

    for cp in outs:
        cp.wait()
    act_own.wait()
    for cp in act:
        cp.wait_recv()
    for cp in list(halo.values()) + w_copies + cot_copies + a2a + ag + act + wx + list(ret.values()):
        cp.wait_send()
    each(1, PLANE, lambda d: rs_copy(d).wait_send())
    each(1, Z, lambda d: z_copy(d).wait_send())
    each(1, PLANE, lambda d: fin_copy(d).wait_send())


def local(D, F, features, weight, cotangent, tile_values, tile_rows, tile_cols, tile_count, send_lists, send_count):
    FR, NODES = features.shape
    H = weight.shape[0]
    T, BLK, _ = tile_values.shape
    NB = NODES // BLK
    _, R, SB = send_lists.shape
    PLANE = min(D, FR * H // 1024)
    Z = D // PLANE
    C = CHUNKS
    ROWS = FR // C
    HALO = R * SB
    NBQ, NQ = NB // F, NODES // F
    cfg = (H, FR, NODES, NB, T, R, SB, D, F, PLANE, Z)
    bf, f32 = jnp.bfloat16, jnp.float32
    V = pltpu.VMEM
    scratch = [
        V((FR, NODES), bf),
        V((NB, FR, BLK), bf),
        V((T, BLK, BLK), bf),
        V((C, HALO, ROWS, BLK), bf),
        V((C, F, ROWS, NQ), bf),
        V((H, NQ), bf),
        V((H, NQ), bf),
        V((F, H, FR), bf),
        V((H, H), bf),
        V((H, H), bf),
        V((H, NQ), bf),
        V((F, FR, NQ), bf),
        V((C, F, NBQ, ROWS, BLK), bf),
    ]
    scratch += [V((NB + HALO, ROWS, BLK), bf) for _ in range(C)]
    scratch += [V((NB, ROWS, BLK), bf) for _ in range(C)]
    scratch += [V((T, ROWS, BLK), f32), V((C, HALO, ROWS, BLK), bf)]
    scratch += [V((HALO, ROWS, BLK), bf) for _ in range(C)]
    scratch += [
        V((HALO, ROWS, BLK), f32),
        V((C, NB, ROWS, BLK), f32),
        V((F, FR, H), f32),
        V((F, FR, H), f32),
        V((PLANE, 8, LANES), f32),
        V((PLANE, 8, LANES), f32),
        V((Z, 8, LANES), f32),
        V((PLANE, 8, LANES), f32),
        V((16, LANES), jnp.int32),
        pltpu.SMEM((16, LANES), jnp.int32),
    ]
    sem = pltpu.SemaphoreType.DMA
    scratch += [
        sem((6 + 3 * C,)),
        sem((2, C * R)),
        sem((2, C * F)),
        sem((2, F)),
        sem((2, F)),
        sem((2, F)),
        sem((2, C * F)),
        sem((2, C * R)),
        sem((2, F)),
        sem((2, PLANE)),
        sem((2, Z)),
        sem((2, PLANE)),
    ]
    any_spec = pl.BlockSpec(memory_space=pl.ANY)
    smem = pl.BlockSpec(memory_space=pltpu.SMEM)
    return pl.pallas_call(
        functools.partial(kernel, cfg),
        out_shape=(
            jax.ShapeDtypeStruct((FR, NODES), bf),
            jax.ShapeDtypeStruct((H, FR), f32),
            jax.ShapeDtypeStruct((FR, NODES), bf),
        ),
        in_specs=[any_spec] * 4 + [smem] * 5,
        out_specs=(any_spec, pl.BlockSpec(memory_space=pltpu.VMEM), any_spec),
        scratch_shapes=scratch,
        compiler_params=pltpu.CompilerParams(
            collective_id=0, has_side_effects=True, vmem_limit_bytes=48 * 1024 * 1024
        ),
    )(features, weight, cotangent, tile_values, tile_rows, tile_cols, tile_count, send_lists, send_count)


def solution(mesh):
    return jax.shard_map(
        functools.partial(local, mesh.shape["dom"], mesh.shape["feat"]),
        mesh=mesh,
        in_specs=(
            P("feat", "dom"),
            P(None, "feat"),
            P("feat", "dom"),
            P("dom", None, None),
            P("dom"),
            P("dom"),
            P("dom"),
            P("dom", None, None),
            P("dom", None),
        ),
        out_specs=(P("feat", "dom"), P(None, "feat"), P("feat", "dom")),
        check_vma=False,
    )
```

time: 379 us -> 79 us (0.21)
  waiting for transfers between devices: 235 us -> 0 us
  Pallas kernels: 0 us -> 67.9 us
  starting transfers between devices: 53.8 us -> 0 us
  matrix products: 24.9 us -> 0 us
  local copies, waits for them, and re-layouts: 31.5 us -> 9.43 us
  other arithmetic: 17.9 us -> 0 us
  between operations: 14.9 us -> 1.3 us
    psum x1 -> x0, waiting for transfers between devices: 170 us -> none  [local(): lax.psum(weight_part, 'dom') / jnp.sqrt(jnp.float32(total_nodes))]
    pallas_call x0 -> x1, Pallas kernels: none -> 67.9 us  [local(): pl.pallas_call(functools.partial(kernel, cfg), out_shape=(jax.ShapeDtypeS...]
    ppermute x14 -> x0, starting transfers between devices: 53.7 us -> none  [swapped(): lax.ppermute(x, axis, [(i, i ^ 1 << distance) for i in range(lax.axis_siz...]
    unnamed x4 -> x0, waiting for transfers between devices: 25.3 us -> none
    dot_general x16 -> x0, matrix products: 24.9 us -> none  [the longest x7 6.66 us: local(): jnp.einsum('fjc,jk->fkc', returned, place_onehot, precision=highest)]
    all_gather x1 -> x0, waiting for transfers between devices: 23.8 us -> none  [local(): full_agg = lax.all_gather(aggregated, 'feat', axis=0, tiled=True)]
    ppermute x14 -> x0, waiting for transfers between devices: 16.1 us -> none  [swapped(): lax.ppermute(x, axis, [(i, i ^ 1 << distance) for i in range(lax.axis_siz...]
    gather x9 -> x0, local copies, waits for them, and re-layouts: 9.87 us -> none  [the longest x7 4.63 us: local(): jnp.take(blocks, lists[level], axis=1)]
  transfers between devices with their start and end apart: 17 -> 0, of which waited for: 6 -> 0; matrix products, arithmetic and copies ran while one was open for 13% -> 0% of each run, Pallas kernels for 0% -> 0%
where the time goes in v1:
time: 79 us; the launch traced here: 78.6 us
  Pallas kernels  67.9 us (86%)
  local copies, waits for them, and re-layouts  9.43 us (12%)
  between operations  1.3 us (2%)
    pallas_call x1, Pallas kernels, local(): pl.pallas_call(functools.partial(kernel, cfg), out_shape=(jax.ShapeDtypeS...  67.9 us
    unnamed x16, local copies, waits for them, and re-layouts  8.71 us

profile of v1, /device:TPU:1, one launch (start us, length us, event | category | flops | bytes accessed | tf_op | source)
XLA Modules:
  0.0 78.6 jit_solution(3619662484803695849)
XLA Ops:
  1.3 0.7 copy.13.lists_s
  2.0 0.9 %copy.12.w_hbm = bf16[256,64]{1,0:T(8,128)(2,1)S(1)} copy(bf16[256,64]{0,1:T(8,128)(2,1)} %param.10) | data formatting | bytes 65536 | tf_op args[1]
  2.8 0.0 copy-start
  2.8 1.9 %copy-done = bf16[96,128,128]{2,1,0:T(8,128)(2,1)S(1)} copy-done((bf16[96,128,128]{2,1,0:T(8,128)(2,1)S(1)}, bf16[96,128,128]{2,1,0:T(8,128)(2,1)}, u32[]{:S(2)}) %copy-start) | copy-done | bytes 3145752
  4.7 0.0 copy-start.1
  4.7 0.9 %copy-done.1 = bf16[64,2048]{1,0:T(8,128)(2,1)S(1)} copy-done((bf16[64,2048]{1,0:T(8,128)(2,1)S(1)}, bf16[64,2048]{1,0:T(8,128)(2,1)}, u32[]{:S(2)}) %copy-start.1) | copy-done | bytes 262168
  5.7 0.0 copy-start.2
  5.7 0.9 %copy-done.2 = bf16[64,2048]{1,0:T(8,128)(2,1)S(1)} copy-done((bf16[64,2048]{1,0:T(8,128)(2,1)S(1)}, bf16[64,2048]{1,0:T(8,128)(2,1)}, u32[]{:S(2)}) %copy-start.2) | copy-done | bytes 262168
  6.6 0.0 copy-start.3
  6.6 0.7 copy-done.3
  7.3 0.0 copy-start.4
  7.3 0.7 copy-done.4
  7.9 0.0 copy-start.5
  7.9 0.7 copy-done.5
  8.6 67.9 %shard_map.112 = (bf16[64,2048]{1,0:T(8,128)(2,1)S(1)}, f32[256,64]{1,0:T(8,128)S(1)}, bf16[64,2048]{1,0:T(8,128)(2,1)S(1)}) custom-call(bf16[64,2048]{1,0:T(8,128)(2,1)S(1)} %copy-done.1, bf16[256,64]{1,0:T(8,128)(2,1)S(1)} %copy.12.w_hbm, bf16[64,2048]{1,0:T(8,128)(2,1)S(1)} %copy-done.2, bf16[96,128,128]{2,1,0:T(8,128)(2,1)S(1)} %copy-done, ...), custom_call_target="tpu_custom_call" | custom-call | tf_op jit(solution)/shard_map/pallas_call | solution.py:553
  76.5 0.7 copy.14
  77.2 0.7 copy.18
  77.9 0.7 copy.19
Async XLA Ops:
  2.8 1.9 %copy-start = (bf16[96,128,128]{2,1,0:T(8,128)(2,1)S(1)}, bf16[96,128,128]{2,1,0:T(8,128)(2,1)}, u32[]{:S(2)}) copy-start(bf16[96,128,128]{2,1,0:T(8,128)(2,1)} %tiles_hbm.1) | copy-start | bytes 9437188
  4.7 0.9 %copy-start.1 = (bf16[64,2048]{1,0:T(8,128)(2,1)S(1)}, bf16[64,2048]{1,0:T(8,128)(2,1)}, u32[]{:S(2)}) copy-start(bf16[64,2048]{1,0:T(8,128)(2,1)} %x_hbm.1) | copy-start | bytes 786436
  5.7 0.9 %copy-start.2 = (bf16[64,2048]{1,0:T(8,128)(2,1)S(1)}, bf16[64,2048]{1,0:T(8,128)(2,1)}, u32[]{:S(2)}) copy-start(bf16[64,2048]{1,0:T(8,128)(2,1)} %cot_hbm.1) | copy-start | bytes 786436
  6.6 0.7 copy-start.3
  7.3 0.7 copy-start.4
  7.9 0.7 copy-start.5

commit v2 on v1

--- a/solution.py
+++ b/solution.py
@@ -11,6 +11,7 @@
 CHUNKS = 2
 UNROLL = 8
 LANES = 128
+VMEM_LIMIT = 63 * 1024 * 1024
 GELU_C = 0.7978845608028654
 GELU_A = 0.044715
 F_PERM, F_SRC, F_KEEP, F_LAST, F_HAS = 0, 1, 2, 3, 4
@@ -40,8 +41,8 @@
 
 def kernel(
     cfg,
-    x_hbm, w_hbm, cot_hbm, tiles_hbm, rows_s, cols_s, count_s, lists_s, sc_s,
-    act_hbm, wgrad_ref, fg_hbm,
+    x_hbm, w_hbm, cot_hbm, tiles_hbm, rows_hbm, cols_hbm, count_hbm, lists_hbm, sc_hbm,
+    act_hbm, wgrad_hbm, fg_hbm,
     *scratch,
 ):
     (H, FR, NODES, NB, T, R, SB, D, F, PLANE, Z) = cfg
@@ -57,13 +58,14 @@
         del refs[:n]
         return out
 
-    (xv, xb, tv, snd, aggS, aggG, cotG, wg, wfull, wt, pg, actS, agS) = take(13)
+    (xv, xb, tv, snd, aggS, aggG, cotG, wfull, wt, pg, actS, agS) = take(12)
     src = take(C)
     gb = take(C)
     (buf, ret_s) = take(2)
     ret_r = take(C)
-    (ebuf, fgv, wpS, wxR, wR, rsR, zR, finR, tab_v, tab_s) = take(10)
-    (loc_sem, halo_sem, a2a_sem, w_sem, cot_sem, act_sem, ag_sem, ret_sem, wx_sem, rs_sem, z_sem, fin_sem) = take(12)
+    (ebuf, fgv, wpS, wxR, wR, rsR, zR, finR, wgv, tab_v, tab_s) = take(11)
+    (rows_s, cols_s, count_s, lists_s, sc_s) = take(5)
+    (in_sem, loc_sem, halo_sem, a2a_sem, w_sem, cot_sem, act_sem, ag_sem, ret_sem, wx_sem, rs_sem, z_sem, fin_sem) = take(13)
 
     dom = lax.axis_index("dom")
     me = lax.axis_index("feat")
@@ -93,6 +95,12 @@
 
     lax.fori_loop(1, Z, hello_z, 0)
 
+    small = []
+    for i, (a, b) in enumerate(
+        ((lists_hbm, lists_s), (sc_hbm, sc_s), (rows_hbm, rows_s), (cols_hbm, cols_s), (count_hbm, count_s))
+    ):
+        small.append(pltpu.make_async_copy(a, b, in_sem.at[i]))
+        small[-1].start()
     load_x = pltpu.make_async_copy(x_hbm, xv, loc_sem.at[0])
     load_x.start()
     load_t = pltpu.make_async_copy(tiles_hbm, tv, loc_sem.at[1])
@@ -103,9 +111,12 @@
         loc_sem.at[2],
     )
     own_cot.start()
-    own_w = pltpu.make_async_copy(w_hbm, wg.at[me], loc_sem.at[3])
+    own_rows = pl.ds(pl.multiple_of(me * FR, 16), FR)
+    own_w = pltpu.make_async_copy(w_hbm, wt.at[own_rows, :], loc_sem.at[3])
     own_w.start()
     load_x.wait()
+    for cp in small:
+        cp.wait()
 
     for k in range(NB):
         xb[k] = xv[:, k * LANES : (k + 1) * LANES]
@@ -114,7 +125,7 @@
 
         def fill(j, c, b=b):
             live = (zero_block + j < sc_s[0, b]).astype(jnp.float32)
-            block = (xb[lists_s[0, b, j]].astype(jnp.float32) * live).astype(jnp.bfloat16)
+            block = (xb[lists_s[b, 0, j]].astype(jnp.float32) * live).astype(jnp.bfloat16)
             for h in range(C):
                 snd[h, b * SB + j] = block[h * ROWS : (h + 1) * ROWS]
             return c
@@ -152,7 +163,7 @@
         q = feat_peer(d)
         cp = pltpu.make_async_remote_copy(
             src_ref=w_hbm,
-            dst_ref=wg.at[me],
+            dst_ref=wt.at[own_rows, :],
             send_sem=w_sem.at[0, d],
             recv_sem=w_sem.at[1, d],
             device_id=(dom, q),
@@ -188,7 +199,7 @@
     for b in range(R):
 
         def read_entry(j, c, b=b):
-            return jnp.where((lane == b * SB + j) & (zero_row + j < sc_s[0, b]), lists_s[0, b, j], c)
+            return jnp.where((lane == b * SB + j) & (zero_row + j < sc_s[0, b]), lists_s[b, 0, j], c)
 
         list_v = lax.fori_loop(0, SB, read_entry, list_v)
     dead = lane >= count_s[0]
@@ -211,9 +222,7 @@
     own_w.wait()
     for cp in w_copies:
         cp.wait_recv()
-    wall = jnp.concatenate([wg[q].astype(jnp.float32) for q in range(F)], axis=1)
-    wfull[...] = wall.astype(jnp.bfloat16)
-    wt[...] = jnp.transpose(wall).astype(jnp.bfloat16)
+    wfull[...] = jnp.transpose(wt[...].astype(jnp.float32)).astype(jnp.bfloat16)
 
     table.wait()
     load_t.wait()
@@ -413,6 +422,8 @@
         finR[m] = total * (float(NODES * D) ** -0.5)
         each(1, PLANE, lambda d: fin_copy(d).start())
 
+    out_w = pltpu.make_async_copy(wgv, wgrad_hbm, in_sem.at[5])
+
     def finish_weight():
         each(1, PLANE, lambda d: fin_copy(d).wait_recv())
         whole = jnp.concatenate(
@@ -422,7 +433,8 @@
             ],
             axis=0,
         )
-        wgrad_ref[...] = jnp.transpose(whole)
+        wgv[...] = whole
+        out_w.start()
 
     def ret_copy(h, b):
         return pltpu.make_async_remote_copy(
@@ -477,6 +489,7 @@
 
     for cp in outs:
         cp.wait()
+    out_w.wait()
     act_own.wait()
     for cp in act:
         cp.wait_recv()
@@ -510,7 +523,6 @@
         V((C, F, ROWS, NQ), bf),
         V((H, NQ), bf),
         V((H, NQ), bf),
-        V((F, H, FR), bf),
         V((H, H), bf),
         V((H, H), bf),
         V((H, NQ), bf),
@@ -530,11 +542,18 @@
         V((PLANE, 8, LANES), f32),
         V((Z, 8, LANES), f32),
         V((PLANE, 8, LANES), f32),
+        V((FR, H), f32),
         V((16, LANES), jnp.int32),
         pltpu.SMEM((16, LANES), jnp.int32),
+        pltpu.SMEM((T,), jnp.int32),
+        pltpu.SMEM((T,), jnp.int32),
+        pltpu.SMEM((1,), jnp.int32),
+        pltpu.SMEM((R, 1, SB), jnp.int32),
+        pltpu.SMEM((1, R), jnp.int32),
     ]
     sem = pltpu.SemaphoreType.DMA
     scratch += [
+        sem((6,)),
         sem((6 + 3 * C,)),
         sem((2, C * R)),
         sem((2, C * F)),
@@ -549,21 +568,31 @@
         sem((2, PLANE)),
     ]
     any_spec = pl.BlockSpec(memory_space=pl.ANY)
-    smem = pl.BlockSpec(memory_space=pltpu.SMEM)
-    return pl.pallas_call(
+    act, wgrad, fgrad = pl.pallas_call(
         functools.partial(kernel, cfg),
         out_shape=(
             jax.ShapeDtypeStruct((FR, NODES), bf),
-            jax.ShapeDtypeStruct((H, FR), f32),
+            jax.ShapeDtypeStruct((FR, H), f32),
             jax.ShapeDtypeStruct((FR, NODES), bf),
         ),
-        in_specs=[any_spec] * 4 + [smem] * 5,
-        out_specs=(any_spec, pl.BlockSpec(memory_space=pltpu.VMEM), any_spec),
+        in_specs=[any_spec] * 9,
+        out_specs=(any_spec,) * 3,
         scratch_shapes=scratch,
         compiler_params=pltpu.CompilerParams(
-            collective_id=0, has_side_effects=True, vmem_limit_bytes=48 * 1024 * 1024
+            collective_id=0, has_side_effects=True, vmem_limit_bytes=VMEM_LIMIT
         ),
-    )(features, weight, cotangent, tile_values, tile_rows, tile_cols, tile_count, send_lists, send_count)
+    )(
+        features,
+        weight.T,
+        cotangent,
+        tile_values,
+        tile_rows,
+        tile_cols,
+        tile_count,
+        jnp.transpose(send_lists, (1, 0, 2)),
+        send_count,
+    )
+    return act, wgrad.T, fgrad
 
 
 def solution(mesh):

time: 79 us -> 74.1 us (0.938)
  local copies, waits for them, and re-layouts: 9.43 us -> 4.81 us
    unnamed x16 -> x3, local copies, waits for them, and re-layouts: 8.71 us -> 4.81 us
where the time goes in v2:
time: 74.1 us; the launch traced here: 73.9 us
  Pallas kernels  67.8 us (91%)
  local copies, waits for them, and re-layouts  4.81 us (6%)
  between operations  1.29 us (2%)
    pallas_call x1, Pallas kernels, local(): pl.pallas_call(functools.partial(kernel, cfg), out_shape=(jax.ShapeDtypeS...  67.8 us
    unnamed x3, local copies, waits for them, and re-layouts  4.81 us

profile of v2, /device:TPU:1, one launch (start us, length us, event | category | flops | bytes accessed | tf_op | source)
XLA Modules:
  0.0 73.9 jit_solution(13178215381281962484)
XLA Ops:
  1.3 67.8 %shard_map.112 = (bf16[64,2048]{1,0:T(8,128)(2,1)}, f32[64,256]{1,0:T(8,128)}, bf16[64,2048]{1,0:T(8,128)(2,1)}) custom-call(bf16[64,2048]{1,0:T(8,128)(2,1)} %x_hbm.1, bf16[64,256]{1,0:T(8,128)(2,1)} %bitcast.4, bf16[64,2048]{1,0:T(8,128)(2,1)} %cot_hbm.1, bf16[96,128,128]{2,1,0:T(8,128)(2,1)} %tiles_hbm.1, s32[96]{0:T(128)} %rows_hbm.1, s32[96]{0:T(128)} %cols_hbm.1, ...), custom_call_target="tpu_custom_call" | custom-call | tf_op jit(solution)/shard_map/pallas_call | solution.py:571
  69.1 1.7 %copy.16 = bf16[64,2048]{1,0:T(8,128)(2,1)} copy(bf16[64,2048]{1,0:T(8,128)(2,1)} %get-tuple-element.12) | data formatting | bytes 524288
  70.7 1.5 %copy.17 = f32[256,64]{0,1:T(8,128)} copy(f32[256,64]{0,1:T(8,128)} %bitcast.3) | data formatting | bytes 131072
  72.2 1.7 %copy.18 = bf16[64,2048]{1,0:T(8,128)(2,1)} copy(bf16[64,2048]{1,0:T(8,128)(2,1)} %get-tuple-element.14) | data formatting | bytes 524288

commit v3 on v2

--- a/solution.py
+++ b/solution.py
@@ -75,36 +75,14 @@
     def dom_at(mm, zz):
         return zz * PLANE + mm
 
-    barrier = pltpu.get_barrier_semaphore()
-    for d in range(1, F):
-        pl.semaphore_signal(barrier, inc=1, device_id=(dom, lax.rem(me + d, F)), device_id_type=MESH)
-
-    def hello_plane(d, c):
-        pl.semaphore_signal(
-            barrier, inc=1, device_id=(dom_at(lax.rem(m + d, PLANE), zi), me), device_id_type=MESH
-        )
-        return c
-
-    lax.fori_loop(1, PLANE, hello_plane, 0)
-
-    def hello_z(d, c):
-        pl.semaphore_signal(
-            barrier, inc=1, device_id=(dom_at(m, lax.rem(zi + d, Z)), me), device_id_type=MESH
-        )
-        return c
-
-    lax.fori_loop(1, Z, hello_z, 0)
-
+    load_x = pltpu.make_async_copy(x_hbm, xv, loc_sem.at[0])
+    load_x.start()
     small = []
     for i, (a, b) in enumerate(
         ((lists_hbm, lists_s), (sc_hbm, sc_s), (rows_hbm, rows_s), (cols_hbm, cols_s), (count_hbm, count_s))
     ):
         small.append(pltpu.make_async_copy(a, b, in_sem.at[i]))
         small[-1].start()
-    load_x = pltpu.make_async_copy(x_hbm, xv, loc_sem.at[0])
-    load_x.start()
-    load_t = pltpu.make_async_copy(tiles_hbm, tv, loc_sem.at[1])
-    load_t.start()
     own_cot = pltpu.make_async_copy(
         cot_hbm.at[:, pl.ds(pl.multiple_of(me * NQ, LANES), NQ)],
         cotG.at[pl.ds(pl.multiple_of(me * FR, 16), FR), :],
@@ -114,7 +92,30 @@
     own_rows = pl.ds(pl.multiple_of(me * FR, 16), FR)
     own_w = pltpu.make_async_copy(w_hbm, wt.at[own_rows, :], loc_sem.at[3])
     own_w.start()
+
+    barrier = pltpu.get_barrier_semaphore()
+    for d in range(1, F):
+        pl.semaphore_signal(barrier, inc=1, device_id=(dom, lax.rem(me + d, F)), device_id_type=MESH)
+
+    def hello_plane(d, c):
+        pl.semaphore_signal(
+            barrier, inc=1, device_id=(dom_at(lax.rem(m + d, PLANE), zi), me), device_id_type=MESH
+        )
+        return c
+
+    lax.fori_loop(1, PLANE, hello_plane, 0)
+
+    def hello_z(d, c):
+        pl.semaphore_signal(
+            barrier, inc=1, device_id=(dom_at(m, lax.rem(zi + d, Z)), me), device_id_type=MESH
+        )
+        return c
+
+    lax.fori_loop(1, Z, hello_z, 0)
+
     load_x.wait()
+    load_t = pltpu.make_async_copy(tiles_hbm, tv, loc_sem.at[1])
+    load_t.start()
     for cp in small:
         cp.wait()
 
@@ -130,7 +131,7 @@
                 snd[h, b * SB + j] = block[h * ROWS : (h + 1) * ROWS]
             return c
 
-        lax.fori_loop(0, SB, fill, 0)
+        lax.fori_loop(0, SB, fill, 0, unroll=True)
 
     pl.semaphore_wait(barrier, (F - 1) + (PLANE - 1) + (Z - 1))
 
@@ -280,8 +281,8 @@
     for cp in a2a:
         cp.wait_recv()
 
-    def dense(q, c):
-        here = pl.ds(pl.multiple_of(q * FR, 16), FR)
+    for q in range(F):
+        here = slice(q * FR, (q + 1) * FR)
         pre = jnp.dot(wt[here, :], aggG[...], preferred_element_type=jnp.float32)
         square = pre * pre
         t = jnp.tanh(GELU_C * pre * (1.0 + GELU_A * square))
@@ -289,21 +290,35 @@
         actS[q] = (pre * half).astype(jnp.bfloat16)
         slope = half + (0.5 * GELU_C) * pre * (1.0 - t * t) * (1.0 + (3.0 * GELU_A) * square)
         pg[here, :] = (cotG[here, :].astype(jnp.float32) * slope).astype(jnp.bfloat16)
+
+    def weight_term(q, c):
+        here = pl.ds(pl.multiple_of(q * FR, 16), FR)
+        wpS[q] = lax.dot_general(
+            pg[here, :], aggG[...], (((1,), (1,)), ((), ())), preferred_element_type=jnp.float32
+        ).astype(jnp.bfloat16)
         return c
 
-    lax.fori_loop(0, F, dense, 0)
+    lax.fori_loop(0, F, weight_term, 0)
+    wx = []
+    for d in range(1, F):
+        cp = pltpu.make_async_remote_copy(
+            src_ref=wpS.at[feat_peer(d)],
+            dst_ref=wxR.at[d],
+            send_sem=wx_sem.at[0, d],
+            recv_sem=wx_sem.at[1, d],
+            device_id=(dom, feat_peer(d)),
+            device_id_type=MESH,
+        )
+        cp.start()
+        wx.append(cp)
 
     ag, ag_own = [], []
     for h in range(C):
-
-        def agg_grad(q, c, h=h):
-            here = pl.ds(pl.multiple_of(q * FR + h * ROWS, 16), ROWS)
+        for q in range(F):
+            here = slice(q * FR + h * ROWS, q * FR + (h + 1) * ROWS)
             g = jnp.dot(wfull[here, :], pg[...], preferred_element_type=jnp.float32).astype(jnp.bfloat16)
             for k in range(NBQ):
                 agS[h, q, k] = g[:, k * LANES : (k + 1) * LANES]
-            return c
-
-        lax.fori_loop(0, F, agg_grad, 0)
         place = pl.ds(me * NBQ, NBQ)
         for d in range(1, F):
             q = feat_peer(d)
@@ -338,27 +353,6 @@
     act_own = pltpu.make_async_copy(actS.at[me], act_hbm.at[:, place], loc_sem.at[5 + 2 * C])
     act_own.start()
 
-    def weight_term(q, c):
-        here = pl.ds(pl.multiple_of(q * FR, 16), FR)
-        wpS[q] = lax.dot_general(
-            pg[here, :], aggG[...], (((1,), (1,)), ((), ())), preferred_element_type=jnp.float32
-        )
-        return c
-
-    lax.fori_loop(0, F, weight_term, 0)
-    wx = []
-    for d in range(1, F):
-        cp = pltpu.make_async_remote_copy(
-            src_ref=wpS.at[feat_peer(d)],
-            dst_ref=wxR.at[d],
-            send_sem=wx_sem.at[0, d],
-            recv_sem=wx_sem.at[1, d],
-            device_id=(dom, feat_peer(d)),
-            device_id_type=MESH,
-        )
-        cp.start()
-        wx.append(cp)
-
     def plane_copy(d, from_ref, to_ref, sem):
         mm = lax.rem(m + d, PLANE)
         return pltpu.make_async_remote_copy(
@@ -386,46 +380,50 @@
             device_id_type=MESH,
         )
 
-    def each(low, high, act_on):
-        def body(d, c):
-            act_on(d)
-            return c
-
-        lax.fori_loop(low, high, body, 0)
+    rs, zs, fin = [], [], []
 
     across = H // LANES
 
     def reduce_feat():
         for cp in wx:
             cp.wait_recv()
-        total = wpS[me]
+        total = wpS[me].astype(jnp.float32)
         for d in range(1, F):
-            total = total + wxR[d]
+            total = total + wxR[d].astype(jnp.float32)
         for p in range(PLANE):
             wR[p] = total[8 * (p // across) : 8 * (p // across) + 8, LANES * (p % across) : LANES * (p % across + 1)]
-        each(1, PLANE, lambda d: rs_copy(d).start())
+        for d in range(1, PLANE):
+            rs.append(rs_copy(d))
+            rs[-1].start()
 
     def reduce_plane():
         rsR[m] = wR[m]
-        each(1, PLANE, lambda d: rs_copy(d).wait_recv())
+        for cp in rs:
+            cp.wait_recv()
         total = rsR[0]
         for p in range(1, PLANE):
             total = total + rsR[p]
         zR[zi] = total
-        each(1, Z, lambda d: z_copy(d).start())
+        for d in range(1, Z):
+            zs.append(z_copy(d))
+            zs[-1].start()
 
     def reduce_z():
-        each(1, Z, lambda d: z_copy(d).wait_recv())
+        for cp in zs:
+            cp.wait_recv()
         total = zR[0]
         for p in range(1, Z):
             total = total + zR[p]
         finR[m] = total * (float(NODES * D) ** -0.5)
-        each(1, PLANE, lambda d: fin_copy(d).start())
+        for d in range(1, PLANE):
+            fin.append(fin_copy(d))
+            fin[-1].start()
 
     out_w = pltpu.make_async_copy(wgv, wgrad_hbm, in_sem.at[5])
 
     def finish_weight():
-        each(1, PLANE, lambda d: fin_copy(d).wait_recv())
+        for cp in fin:
+            cp.wait_recv()
         whole = jnp.concatenate(
             [
                 jnp.concatenate([finR[r * across + a] for a in range(across)], axis=1)
@@ -447,6 +445,7 @@
         )
 
     ret = {}
+    reduce_feat()
     for h in range(C):
         ag_own[h].wait()
         for cp in ag[h * (F - 1) : (h + 1) * (F - 1)]:
@@ -461,9 +460,9 @@
         for k in range(NB):
             fgv[h, k] = segment(buf, B_LAST, B_HAS, k)
         if h == 0:
-            reduce_feat()
-    reduce_plane()
-
+            reduce_plane()
+
+    reduce_z()
     outs = []
     for h in range(C):
         for b in order:
@@ -474,7 +473,7 @@
             ebuf[e] = run
             return run
 
-        lax.fori_loop(0, HALO, gather_entry, jnp.zeros((ROWS, LANES), jnp.float32))
+        lax.fori_loop(0, HALO, gather_entry, jnp.zeros((ROWS, LANES), jnp.float32), unroll=8)
         for k in range(NB):
             xv[h * ROWS : (h + 1) * ROWS, k * LANES : (k + 1) * LANES] = (
                 fgv[h, k] + segment(ebuf, E_LAST, E_HAS, k)
@@ -483,8 +482,6 @@
         cp = pltpu.make_async_copy(xv.at[here, :], fg_hbm.at[here, :], loc_sem.at[6 + 2 * C + h])
         cp.start()
         outs.append(cp)
-        if h == 0:
-            reduce_z()
     finish_weight()
 
     for cp in outs:
@@ -493,11 +490,21 @@
     act_own.wait()
     for cp in act:
         cp.wait_recv()
-    for cp in list(halo.values()) + w_copies + cot_copies + a2a + ag + act + wx + list(ret.values()):
+    for cp in list(halo.values()) + w_copies + cot_copies + a2a + ag + act + wx + list(ret.values()) + rs + zs + fin:
         cp.wait_send()
-    each(1, PLANE, lambda d: rs_copy(d).wait_send())
-    each(1, Z, lambda d: z_copy(d).wait_send())
-    each(1, PLANE, lambda d: fin_copy(d).wait_send())
+
+
+def settle(a, b, c, out_a, out_b, out_c, va, vb, vc, sem):
+    held = ((a, va, out_a), (b, vb, out_b), (c, vc, out_c))
+    loads = [pltpu.make_async_copy(x, v, sem.at[0, i]) for i, (x, v, _) in enumerate(held)]
+    stores = [pltpu.make_async_copy(v, y, sem.at[1, i]) for i, (_, v, y) in enumerate(held)]
+    for cp in loads:
+        cp.start()
+    for load, store in zip(loads, stores):
+        load.wait()
+        store.start()
+    for cp in stores:
+        cp.wait()
 
 
 def local(D, F, features, weight, cotangent, tile_values, tile_rows, tile_cols, tile_count, send_lists, send_count):
@@ -536,8 +543,8 @@
     scratch += [
         V((HALO, ROWS, BLK), f32),
         V((C, NB, ROWS, BLK), f32),
-        V((F, FR, H), f32),
-        V((F, FR, H), f32),
+        V((F, FR, H), bf),
+        V((F, FR, H), bf),
         V((PLANE, 8, LANES), f32),
         V((PLANE, 8, LANES), f32),
         V((Z, 8, LANES), f32),
@@ -592,6 +599,14 @@
         jnp.transpose(send_lists, (1, 0, 2)),
         send_count,
     )
+    act, wgrad, fgrad = pl.pallas_call(
+        settle,
+        out_shape=tuple(jax.ShapeDtypeStruct(a.shape, a.dtype) for a in (act, wgrad, fgrad)),
+        in_specs=[any_spec] * 3,
+        out_specs=(any_spec,) * 3,
+        scratch_shapes=[V((FR, NODES), bf), V((FR, H), f32), V((FR, NODES), bf), sem((2, 3))],
+        compiler_params=pltpu.CompilerParams(vmem_limit_bytes=VMEM_LIMIT),
+    )(act, wgrad, fgrad)
     return act, wgrad.T, fgrad
 
 

time: 74.1 us -> 65 us (0.88)
  local copies, waits for them, and re-layouts: 4.81 us -> 0 us
  Pallas kernels: 67.8 us -> 63.5 us
    pallas_call x1, Pallas kernels: 67.8 us -> 61.7 us  [local(): pl.pallas_call(functools.partial(kernel, cfg), out_shape=(jax.ShapeDtypeS...]
    unnamed x3 -> x0, local copies, waits for them, and re-layouts: 4.81 us -> none
    pallas_call x0 -> x1, Pallas kernels: none -> 1.82 us  [local(): pl.pallas_call(settle, out_shape=tuple((jax.ShapeDtypeStruct(a.shape, a.d...]
where the time goes in v3:
time: 65 us; the launch traced here: 64.8 us
  Pallas kernels  63.5 us (98%)
  between operations  1.29 us (2%)
    pallas_call x1, Pallas kernels, local(): pl.pallas_call(functools.partial(kernel, cfg), out_shape=(jax.ShapeDtypeS...  61.7 us
    pallas_call x1, Pallas kernels, local(): pl.pallas_call(settle, out_shape=tuple((jax.ShapeDtypeStruct(a.shape, a.d...  1.82 us

profile of v3, /device:TPU:1, one launch (start us, length us, event | category | flops | bytes accessed | tf_op | source)
XLA Modules:
  0.0 64.8 jit_solution(5066905551439251798)
XLA Ops:
  1.3 61.7 %shard_map.112 = (bf16[64,2048]{1,0:T(8,128)(2,1)}, f32[64,256]{1,0:T(8,128)}, bf16[64,2048]{1,0:T(8,128)(2,1)}) custom-call(bf16[64,2048]{1,0:T(8,128)(2,1)} %x_hbm.1, bf16[64,256]{1,0:T(8,128)(2,1)} %bitcast.3, bf16[64,2048]{1,0:T(8,128)(2,1)} %cot_hbm.1, bf16[96,128,128]{2,1,0:T(8,128)(2,1)} %tiles_hbm.1, s32[96]{0:T(128)} %rows_hbm.1, s32[96]{0:T(128)} %cols_hbm.1, ...), custom_call_target="tpu_custom_call" | custom-call | tf_op jit(solution)/shard_map/pallas_call | solution.py:578
  63.0 1.8 %shard_map.113 = (bf16[64,2048]{1,0:T(8,128)(2,1)}, f32[64,256]{1,0:T(8,128)}, bf16[64,2048]{1,0:T(8,128)(2,1)}) custom-call(bf16[64,2048]{1,0:T(8,128)(2,1)} %get-tuple-element.9.a, f32[64,256]{1,0:T(8,128)} %get-tuple-element.10.b, bf16[64,2048]{1,0:T(8,128)(2,1)} %get-tuple-element.11.c), custom_call_target="tpu_custom_call" | custom-call | tf_op jit(solution)/shard_map/pallas_call | solution.py:602

commit v4 on v3

--- a/solution.py
+++ b/solution.py
@@ -9,7 +9,7 @@
 
 MESH = pl.DeviceIdType.MESH
 CHUNKS = 2
-UNROLL = 8
+UNROLL = 48
 LANES = 128
 VMEM_LIMIT = 63 * 1024 * 1024
 GELU_C = 0.7978845608028654
@@ -45,10 +45,11 @@
     act_hbm, wgrad_hbm, fg_hbm,
     *scratch,
 ):
-    (H, FR, NODES, NB, T, R, SB, D, F, PLANE, Z) = cfg
+    (H, FR, NODES, NB, T, R, SB, D, F, Y, Z) = cfg
     C = CHUNKS
     ROWS = FR // C
     HALO = R * SB
+    HF = FR // 2
     NBQ = NB // F
     NQ = NODES // F
     refs = list(scratch)
@@ -63,17 +64,18 @@
     gb = take(C)
     (buf, ret_s) = take(2)
     ret_r = take(C)
-    (ebuf, fgv, wpS, wxR, wR, rsR, zR, finR, wgv, tab_v, tab_s) = take(11)
+    (ebuf, fgv, wpS, wxR, yR, zR, wgv, tab_v, tab_s) = take(9)
     (rows_s, cols_s, count_s, lists_s, sc_s) = take(5)
-    (in_sem, loc_sem, halo_sem, a2a_sem, w_sem, cot_sem, act_sem, ag_sem, ret_sem, wx_sem, rs_sem, z_sem, fin_sem) = take(13)
+    (in_sem, loc_sem, halo_sem, a2a_sem, w_sem, cot_sem, act_sem, ag_sem, ret_sem, wx_sem, y_sem, z_sem, fin_sem) = take(13)
 
     dom = lax.axis_index("dom")
     me = lax.axis_index("feat")
-    m = lax.rem(dom, PLANE)
-    zi = dom // PLANE
-
-    def dom_at(mm, zz):
-        return zz * PLANE + mm
+    core = lax.rem(dom, 2)
+    yi = lax.rem(dom // 2, Y)
+    zi = dom // (2 * Y)
+
+    def dom_at(zz, yy, cc):
+        return (zz * Y + yy) * 2 + cc
 
     load_x = pltpu.make_async_copy(x_hbm, xv, loc_sem.at[0])
     load_x.start()
@@ -94,24 +96,22 @@
     own_w.start()
 
     barrier = pltpu.get_barrier_semaphore()
-    for d in range(1, F):
-        pl.semaphore_signal(barrier, inc=1, device_id=(dom, lax.rem(me + d, F)), device_id_type=MESH)
-
-    def hello_plane(d, c):
+    pairs = [(dx, dc) for dx in range(F) for dc in range(2)][1:]
+    for dx, dc in pairs:
         pl.semaphore_signal(
-            barrier, inc=1, device_id=(dom_at(lax.rem(m + d, PLANE), zi), me), device_id_type=MESH
-        )
-        return c
-
-    lax.fori_loop(1, PLANE, hello_plane, 0)
-
-    def hello_z(d, c):
+            barrier,
+            inc=1,
+            device_id=(dom_at(zi, yi, lax.rem(core + dc, 2)), lax.rem(me + dx, F)),
+            device_id_type=MESH,
+        )
+    for d in range(1, Y):
         pl.semaphore_signal(
-            barrier, inc=1, device_id=(dom_at(m, lax.rem(zi + d, Z)), me), device_id_type=MESH
-        )
-        return c
-
-    lax.fori_loop(1, Z, hello_z, 0)
+            barrier, inc=1, device_id=(dom_at(zi, lax.rem(yi + d, Y), core), me), device_id_type=MESH
+        )
+    for d in range(1, Z):
+        pl.semaphore_signal(
+            barrier, inc=1, device_id=(dom_at(lax.rem(zi + d, Z), yi, core), me), device_id_type=MESH
+        )
 
     load_x.wait()
     load_t = pltpu.make_async_copy(tiles_hbm, tv, loc_sem.at[1])
@@ -133,7 +133,7 @@
 
         lax.fori_loop(0, SB, fill, 0, unroll=True)
 
-    pl.semaphore_wait(barrier, (F - 1) + (PLANE - 1) + (Z - 1))
+    pl.semaphore_wait(barrier, len(pairs) + (Y - 1) + (Z - 1))
 
     def halo_copy(h, b):
         return pltpu.make_async_remote_copy(
@@ -228,10 +228,12 @@
     table.wait()
     load_t.wait()
 
+    unroll = UNROLL if T % UNROLL == 0 else T
+
     def tile_pass(source, perm, other, keep, contract):
         def body(i, run):
-            for u in range(UNROLL):
-                t = i * UNROLL + u
+            for u in range(unroll):
+                t = i * unroll + u
                 part = lax.dot_general(
                     source[tab_s[other, t]],
                     tv[tab_s[perm, t]],
@@ -242,7 +244,7 @@
                 buf[t] = run
             return run
 
-        lax.fori_loop(0, T // UNROLL, body, jnp.zeros((ROWS, LANES), jnp.float32))
+        lax.fori_loop(0, T // unroll, body, jnp.zeros((ROWS, LANES), jnp.float32))
 
     def segment(values, last, has, k):
         return values[tab_s[last, k]] * tab_s[has, k].astype(jnp.float32)
@@ -291,29 +293,9 @@
         slope = half + (0.5 * GELU_C) * pre * (1.0 - t * t) * (1.0 + (3.0 * GELU_A) * square)
         pg[here, :] = (cotG[here, :].astype(jnp.float32) * slope).astype(jnp.bfloat16)
 
-    def weight_term(q, c):
-        here = pl.ds(pl.multiple_of(q * FR, 16), FR)
-        wpS[q] = lax.dot_general(
-            pg[here, :], aggG[...], (((1,), (1,)), ((), ())), preferred_element_type=jnp.float32
-        ).astype(jnp.bfloat16)
-        return c
-
-    lax.fori_loop(0, F, weight_term, 0)
-    wx = []
-    for d in range(1, F):
-        cp = pltpu.make_async_remote_copy(
-            src_ref=wpS.at[feat_peer(d)],
-            dst_ref=wxR.at[d],
-            send_sem=wx_sem.at[0, d],
-            recv_sem=wx_sem.at[1, d],
-            device_id=(dom, feat_peer(d)),
-            device_id_type=MESH,
-        )
-        cp.start()
-        wx.append(cp)
-
     ag, ag_own = [], []
-    for h in range(C):
+
+    def send_agg_grad(h):
         for q in range(F):
             here = slice(q * FR + h * ROWS, q * FR + (h + 1) * ROWS)
             g = jnp.dot(wfull[here, :], pg[...], preferred_element_type=jnp.float32).astype(jnp.bfloat16)
@@ -336,102 +318,120 @@
         cp.start()
         ag_own.append(cp)
 
-    place = pl.ds(pl.multiple_of(me * NQ, LANES), NQ)
-    act = []
-    for d in range(1, F):
-        q = feat_peer(d)
-        cp = pltpu.make_async_remote_copy(
-            src_ref=actS.at[q],
-            dst_ref=act_hbm.at[:, place],
-            send_sem=act_sem.at[0, d],
-            recv_sem=act_sem.at[1, d],
-            device_id=(dom, q),
-            device_id_type=MESH,
-        )
-        cp.start()
-        act.append(cp)
-    act_own = pltpu.make_async_copy(actS.at[me], act_hbm.at[:, place], loc_sem.at[5 + 2 * C])
-    act_own.start()
-
-    def plane_copy(d, from_ref, to_ref, sem):
-        mm = lax.rem(m + d, PLANE)
-        return pltpu.make_async_remote_copy(
-            src_ref=from_ref(mm),
-            dst_ref=to_ref.at[m],
-            send_sem=sem.at[0, d],
-            recv_sem=sem.at[1, d],
-            device_id=(dom_at(mm, zi), me),
-            device_id_type=MESH,
-        )
-
-    def rs_copy(d):
-        return plane_copy(d, lambda mm: wR.at[mm], rsR, rs_sem)
-
-    def fin_copy(d):
-        return plane_copy(d, lambda mm: finR.at[m], finR, fin_sem)
-
-    def z_copy(d):
-        return pltpu.make_async_remote_copy(
-            src_ref=zR.at[zi],
-            dst_ref=zR.at[zi],
-            send_sem=z_sem.at[0, d],
-            recv_sem=z_sem.at[1, d],
-            device_id=(dom_at(m, lax.rem(zi + d, Z)), me),
-            device_id_type=MESH,
-        )
-
-    rs, zs, fin = [], [], []
-
-    across = H // LANES
+    wx = []
+
+    def send_weight_term():
+        def weight_term(q, c):
+            here = pl.ds(pl.multiple_of(q * FR, 16), FR)
+            wpS[q] = lax.dot_general(
+                pg[here, :], aggG[...], (((1,), (1,)), ((), ())), preferred_element_type=jnp.float32
+            ).astype(jnp.bfloat16)
+            return c
+
+        lax.fori_loop(0, F, weight_term, 0)
+        for i, (dx, dc) in enumerate(pairs):
+            c2 = lax.rem(core + dc, 2)
+            cp = pltpu.make_async_remote_copy(
+                src_ref=wpS.at[feat_peer(dx), pl.ds(pl.multiple_of(c2 * HF, 16), HF)],
+                dst_ref=wxR.at[i],
+                send_sem=wx_sem.at[0, i],
+                recv_sem=wx_sem.at[1, i],
+                device_id=(dom_at(zi, yi, c2), feat_peer(dx)),
+                device_id_type=MESH,
+            )
+            cp.start()
+            wx.append(cp)
+
+    act, act_own = [], []
+
+    def send_activated():
+        place = pl.ds(pl.multiple_of(me * NQ, LANES), NQ)
+        for d in range(1, F):
+            q = feat_peer(d)
+            cp = pltpu.make_async_remote_copy(
+                src_ref=actS.at[q],
+                dst_ref=act_hbm.at[:, place],
+                send_sem=act_sem.at[0, d],
+                recv_sem=act_sem.at[1, d],
+                device_id=(dom, q),
+                device_id_type=MESH,
+            )
+            cp.start()
+            act.append(cp)
+        own = pltpu.make_async_copy(actS.at[me], act_hbm.at[:, place], loc_sem.at[5 + 2 * C])
+        own.start()
+        act_own.append(own)
+
+    send_agg_grad(0)
+    send_weight_term()
+    for h in range(1, C):
+        send_agg_grad(h)
+    send_activated()
+
+    own_half = pl.ds(pl.multiple_of(core * HF, 16), HF)
+    ys, zs, fin = [], [], []
 
     def reduce_feat():
         for cp in wx:
             cp.wait_recv()
-        total = wpS[me].astype(jnp.float32)
-        for d in range(1, F):
-            total = total + wxR[d].astype(jnp.float32)
-        for p in range(PLANE):
-            wR[p] = total[8 * (p // across) : 8 * (p // across) + 8, LANES * (p % across) : LANES * (p % across + 1)]
-        for d in range(1, PLANE):
-            rs.append(rs_copy(d))
-            rs[-1].start()
-
-    def reduce_plane():
-        rsR[m] = wR[m]
-        for cp in rs:
+        total = wpS[me, own_half].astype(jnp.float32)
+        for i in range(len(pairs)):
+            total = total + wxR[i].astype(jnp.float32)
+        yR[yi] = total.astype(jnp.bfloat16)
+        for d in range(1, Y):
+            cp = pltpu.make_async_remote_copy(
+                src_ref=yR.at[yi],
+                dst_ref=yR.at[yi],
+                send_sem=y_sem.at[0, d],
+                recv_sem=y_sem.at[1, d],
+                device_id=(dom_at(zi, lax.rem(yi + d, Y), core), me),
+                device_id_type=MESH,
+            )
+            cp.start()
+            ys.append(cp)
+
+    def reduce_y():
+        for cp in ys:
             cp.wait_recv()
-        total = rsR[0]
-        for p in range(1, PLANE):
-            total = total + rsR[p]
-        zR[zi] = total
+        total = yR[0].astype(jnp.float32)
+        for p in range(1, Y):
+            total = total + yR[p].astype(jnp.float32)
+        zR[zi] = total.astype(jnp.bfloat16)
         for d in range(1, Z):
-            zs.append(z_copy(d))
-            zs[-1].start()
+            cp = pltpu.make_async_remote_copy(
+                src_ref=zR.at[zi],
+                dst_ref=zR.at[zi],
+                send_sem=z_sem.at[0, d],
+                recv_sem=z_sem.at[1, d],
+                device_id=(dom_at(lax.rem(zi + d, Z), yi, core), me),
+                device_id_type=MESH,
+            )
+            cp.start()
+            zs.append(cp)
 
     def reduce_z():
         for cp in zs:
             cp.wait_recv()
-        total = zR[0]
+        total = zR[0].astype(jnp.float32)
         for p in range(1, Z):
-            total = total + zR[p]
-        finR[m] = total * (float(NODES * D) ** -0.5)
-        for d in range(1, PLANE):
-            fin.append(fin_copy(d))
-            fin[-1].start()
+            total = total + zR[p].astype(jnp.float32)
+        wgv[own_half, :] = total * (float(NODES * D) ** -0.5)
+        cp = pltpu.make_async_remote_copy(
+            src_ref=wgv.at[own_half, :],
+            dst_ref=wgv.at[own_half, :],
+            send_sem=fin_sem.at[0],
+            recv_sem=fin_sem.at[1],
+            device_id=(dom_at(zi, yi, 1 - core), me),
+            device_id_type=MESH,
+        )
+        cp.start()
+        fin.append(cp)
 
     out_w = pltpu.make_async_copy(wgv, wgrad_hbm, in_sem.at[5])
 
     def finish_weight():
         for cp in fin:
             cp.wait_recv()
-        whole = jnp.concatenate(
-            [
-                jnp.concatenate([finR[r * across + a] for a in range(across)], axis=1)
-                for r in range(FR // 8)
-            ],
-            axis=0,
-        )
-        wgv[...] = whole
         out_w.start()
 
     def ret_copy(h, b):
@@ -445,12 +445,19 @@
         )
 
     ret = {}
-    reduce_feat()
+    steps = {"wait 0": reduce_feat, "tiles 1": reduce_y, "sent 1": reduce_z}
+
+    def step(name):
+        if name in steps:
+            steps[name]()
+
     for h in range(C):
+        step(f"wait {h}")
         ag_own[h].wait()
         for cp in ag[h * (F - 1) : (h + 1) * (F - 1)]:
             cp.wait_recv()
         tile_pass(gb[h], B_PERM, B_SRC, B_KEEP, 0)
+        step(f"tiles {h}")
         for b in order:
             for j in range(SB):
                 s = b * SB + j
@@ -459,10 +466,8 @@
             ret[h, b].start()
         for k in range(NB):
             fgv[h, k] = segment(buf, B_LAST, B_HAS, k)
-        if h == 0:
-            reduce_plane()
-
-    reduce_z()
+        step(f"sent {h}")
+
     outs = []
     for h in range(C):
         for b in order:
@@ -482,15 +487,17 @@
         cp = pltpu.make_async_copy(xv.at[here, :], fg_hbm.at[here, :], loc_sem.at[6 + 2 * C + h])
         cp.start()
         outs.append(cp)
+        step(f"final {h}")
     finish_weight()
 
     for cp in outs:
         cp.wait()
     out_w.wait()
-    act_own.wait()
+    for cp in act_own:
+        cp.wait()
     for cp in act:
         cp.wait_recv()
-    for cp in list(halo.values()) + w_copies + cot_copies + a2a + ag + act + wx + list(ret.values()) + rs + zs + fin:
+    for cp in list(halo.values()) + w_copies + cot_copies + a2a + ag + act + wx + list(ret.values()) + ys + zs + fin:
         cp.wait_send()
 
 
@@ -513,13 +520,13 @@
     T, BLK, _ = tile_values.shape
     NB = NODES // BLK
     _, R, SB = send_lists.shape
-    PLANE = min(D, FR * H // 1024)
-    Z = D // PLANE
+    Y = 1 << ((R - 1) // 2)
+    Z = D // (2 * Y)
     C = CHUNKS
     ROWS = FR // C
     HALO = R * SB
     NBQ, NQ = NB // F, NODES // F
-    cfg = (H, FR, NODES, NB, T, R, SB, D, F, PLANE, Z)
+    cfg = (H, FR, NODES, NB, T, R, SB, D, F, Y, Z)
     bf, f32 = jnp.bfloat16, jnp.float32
     V = pltpu.VMEM
     scratch = [
@@ -544,11 +551,9 @@
         V((HALO, ROWS, BLK), f32),
         V((C, NB, ROWS, BLK), f32),
         V((F, FR, H), bf),
-        V((F, FR, H), bf),
-        V((PLANE, 8, LANES), f32),
-        V((PLANE, 8, LANES), f32),
-        V((Z, 8, LANES), f32),
-        V((PLANE, 8, LANES), f32),
+        V((2 * F, FR // 2, H), bf),
+        V((Y, FR // 2, H), bf),
+        V((Z, FR // 2, H), bf),
         V((FR, H), f32),
         V((16, LANES), jnp.int32),
         pltpu.SMEM((16, LANES), jnp.int32),
@@ -569,10 +574,10 @@
         sem((2, F)),
         sem((2, C * F)),
         sem((2, C * R)),
-        sem((2, F)),
-        sem((2, PLANE)),
+        sem((2, 2 * F)),
+        sem((2, Y)),
         sem((2, Z)),
-        sem((2, PLANE)),
+        sem((2,)),
     ]
     any_spec = pl.BlockSpec(memory_space=pl.ANY)
     act, wgrad, fgrad = pl.pallas_call(

time: 65 us -> 64 us (0.985)
  Pallas kernels: 63.5 us -> 62.4 us
    pallas_call x1, Pallas kernels: 61.7 us -> 60.6 us  [local(): pl.pallas_call(functools.partial(kernel, cfg), out_shape=(jax.ShapeDtypeS...]
where the time goes in v4:
time: 64 us; the launch traced here: 63.7 us
  Pallas kernels  62.4 us (98%)
  between operations  1.29 us (2%)
    pallas_call x1, Pallas kernels, local(): pl.pallas_call(functools.partial(kernel, cfg), out_shape=(jax.ShapeDtypeS...  60.6 us
    pallas_call x1, Pallas kernels, local(): pl.pallas_call(settle, out_shape=tuple((jax.ShapeDtypeStruct(a.shape, a.d...  1.82 us

profile of v4, /device:TPU:1, one launch (start us, length us, event | category | flops | bytes accessed | tf_op | source)
XLA Modules:
  0.0 63.7 jit_solution(6169535558747371843)
XLA Ops:
  1.3 60.6 %shard_map.112 = (bf16[64,2048]{1,0:T(8,128)(2,1)}, f32[64,256]{1,0:T(8,128)}, bf16[64,2048]{1,0:T(8,128)(2,1)}) custom-call(bf16[64,2048]{1,0:T(8,128)(2,1)} %x_hbm.1, bf16[64,256]{1,0:T(8,128)(2,1)} %bitcast.3, bf16[64,2048]{1,0:T(8,128)(2,1)} %cot_hbm.1, bf16[96,128,128]{2,1,0:T(8,128)(2,1)} %tiles_hbm.1, s32[96]{0:T(128)} %rows_hbm.1, s32[96]{0:T(128)} %cols_hbm.1, ...), custom_call_target="tpu_custom_call" | custom-call | tf_op jit(solution)/shard_map/pallas_call | solution.py:583
  61.9 1.8 %shard_map.113 = (bf16[64,2048]{1,0:T(8,128)(2,1)}, f32[64,256]{1,0:T(8,128)}, bf16[64,2048]{1,0:T(8,128)(2,1)}) custom-call(bf16[64,2048]{1,0:T(8,128)(2,1)} %get-tuple-element.9.a, f32[64,256]{1,0:T(8,128)} %get-tuple-element.10.b, bf16[64,2048]{1,0:T(8,128)(2,1)} %get-tuple-element.11.c), custom_call_target="tpu_custom_call" | custom-call | tf_op jit(solution)/shard_map/pallas_call | solution.py:607

commit v5 on v4

--- a/solution.py
+++ b/solution.py
@@ -366,7 +366,6 @@
     send_weight_term()
     for h in range(1, C):
         send_agg_grad(h)
-    send_activated()
 
     own_half = pl.ds(pl.multiple_of(core * HF, 16), HF)
     ys, zs, fin = [], [], []
@@ -466,6 +465,8 @@
             ret[h, b].start()
         for k in range(NB):
             fgv[h, k] = segment(buf, B_LAST, B_HAS, k)
+        if h == C - 1:
+            send_activated()
         step(f"sent {h}")
 
     outs = []

time: 64 us -> 63.1 us (0.986)
  Pallas kernels: 62.4 us -> 61.7 us
    pallas_call x1, Pallas kernels: 60.6 us -> 59.9 us  [local(): pl.pallas_call(functools.partial(kernel, cfg), out_shape=(jax.ShapeDtypeS...]
where the time goes in v5:
time: 63.1 us; the launch traced here: 63 us
  Pallas kernels  61.7 us (98%)
  between operations  1.29 us (2%)
    pallas_call x1, Pallas kernels, local(): pl.pallas_call(functools.partial(kernel, cfg), out_shape=(jax.ShapeDtypeS...  59.9 us
    pallas_call x1, Pallas kernels, local(): pl.pallas_call(settle, out_shape=tuple((jax.ShapeDtypeStruct(a.shape, a.d...  1.82 us

profile of v5, /device:TPU:1, one launch (start us, length us, event | category | flops | bytes accessed | tf_op | source)
XLA Modules:
  0.0 63.0 jit_solution(6607699888147698180)
XLA Ops:
  1.3 59.9 %shard_map.112 = (bf16[64,2048]{1,0:T(8,128)(2,1)}, f32[64,256]{1,0:T(8,128)}, bf16[64,2048]{1,0:T(8,128)(2,1)}) custom-call(bf16[64,2048]{1,0:T(8,128)(2,1)} %x_hbm.1, bf16[64,256]{1,0:T(8,128)(2,1)} %bitcast.3, bf16[64,2048]{1,0:T(8,128)(2,1)} %cot_hbm.1, bf16[96,128,128]{2,1,0:T(8,128)(2,1)} %tiles_hbm.1, s32[96]{0:T(128)} %rows_hbm.1, s32[96]{0:T(128)} %cols_hbm.1, ...), custom_call_target="tpu_custom_call" | custom-call | tf_op jit(solution)/shard_map/pallas_call | solution.py:584
  61.2 1.8 %shard_map.113 = (bf16[64,2048]{1,0:T(8,128)(2,1)}, f32[64,256]{1,0:T(8,128)}, bf16[64,2048]{1,0:T(8,128)(2,1)}) custom-call(bf16[64,2048]{1,0:T(8,128)(2,1)} %get-tuple-element.9.a, f32[64,256]{1,0:T(8,128)} %get-tuple-element.10.b, bf16[64,2048]{1,0:T(8,128)(2,1)} %get-tuple-element.11.c), custom_call_target="tpu_custom_call" | custom-call | tf_op jit(solution)/shard_map/pallas_call | solution.py:608

commit v6 on v5

--- a/solution.py
+++ b/solution.py
@@ -328,7 +328,7 @@
             ).astype(jnp.bfloat16)
             return c
 
-        lax.fori_loop(0, F, weight_term, 0)
+        lax.fori_loop(0, F, weight_term, 0, unroll=True)
         for i, (dx, dc) in enumerate(pairs):
             c2 = lax.rem(core + dc, 2)
             cp = pltpu.make_async_remote_copy(

time: 63.1 us -> 63.2 us (level)
  no operation moved by 1% of the time
where the time goes in v6:
time: 63.2 us; the launch traced here: 63 us
  Pallas kernels  61.7 us (98%)
  between operations  1.29 us (2%)
    pallas_call x1, Pallas kernels, local(): pl.pallas_call(functools.partial(kernel, cfg), out_shape=(jax.ShapeDtypeS...  59.9 us
    pallas_call x1, Pallas kernels, local(): pl.pallas_call(settle, out_shape=tuple((jax.ShapeDtypeStruct(a.shape, a.d...  1.82 us

profile of v6, /device:TPU:1, one launch (start us, length us, event | category | flops | bytes accessed | tf_op | source)
XLA Modules:
  0.0 63.0 jit_solution(13539514484276044578)
XLA Ops:
  1.3 59.9 %shard_map.112 = (bf16[64,2048]{1,0:T(8,128)(2,1)}, f32[64,256]{1,0:T(8,128)}, bf16[64,2048]{1,0:T(8,128)(2,1)}) custom-call(bf16[64,2048]{1,0:T(8,128)(2,1)} %x_hbm.1, bf16[64,256]{1,0:T(8,128)(2,1)} %bitcast.3, bf16[64,2048]{1,0:T(8,128)(2,1)} %cot_hbm.1, bf16[96,128,128]{2,1,0:T(8,128)(2,1)} %tiles_hbm.1, s32[96]{0:T(128)} %rows_hbm.1, s32[96]{0:T(128)} %cols_hbm.1, ...), custom_call_target="tpu_custom_call" | custom-call | tf_op jit(solution)/shard_map/pallas_call | solution.py:584
  61.2 1.8 %shard_map.113 = (bf16[64,2048]{1,0:T(8,128)(2,1)}, f32[64,256]{1,0:T(8,128)}, bf16[64,2048]{1,0:T(8,128)(2,1)}) custom-call(bf16[64,2048]{1,0:T(8,128)(2,1)} %get-tuple-element.9.a, f32[64,256]{1,0:T(8,128)} %get-tuple-element.10.b, bf16[64,2048]{1,0:T(8,128)(2,1)} %get-tuple-element.11.c), custom_call_target="tpu_custom_call" | custom-call | tf_op jit(solution)/shard_map/pallas_call | solution.py:608
